TPU v7x, 128 devices: a whole 4x4x4 slice. The times are simulated.
128 devices in a mesh: ha: 4 (over z), wa: 4 (over y), img: 8 (over x, core).
Axes of the slice: x: 4, y: 4, z: 4, core: 2. Of those that a mesh axis runs over, the one named last changes fastest.
Arguments:
- images: bfloat16 [512, 40, 40, 192], P('img', 'ha', 'wa'), may hold values from -6 to 6
- classes: int32 [512], replicated, may hold values from 0 to 2, as said below
- image_counts: int32 [8], replicated, may hold values from 32 to 64, as said below
- entry_kernel: bfloat16 [192, 512], replicated, may hold values from -0.4375 to 0.4375
- entry_gain: float32 [512], replicated, may hold values from 0.5 to 1.5
- entry_shift: float32 [512], replicated, may hold values from -1.8 to 1.8
- group_kernel: bfloat16 [3, 3, 64, 512], replicated, may hold values from -0.25 to 0.25
- group_gain: float32 [512], replicated, may hold values from 0.5 to 1.5
- group_shift: float32 [512], replicated, may hold values from -1.8 to 1.8
- squeeze_weight: bfloat16 [512, 48], replicated, may hold values from -0.5 to 0.5
- squeeze_bias: float32 [48], replicated, may hold values from -3 to 3
- excite_weight: bfloat16 [48, 512], replicated, may hold values from -0.875 to 0.875
- excite_bias: float32 [512], replicated, may hold values from -3 to 3
- output_kernel: bfloat16 [512, 512], replicated, may hold values from -0.25 to 0.25
- output_gain: float32 [512], replicated, may hold values from 0.5 to 1.5
- output_shift: float32 [512], replicated, may hold values from -1.8 to 1.8
- shortcut_kernel: bfloat16 [192, 512], replicated, may hold values from -0.4375 to 0.4375
- shortcut_gain: float32 [512], replicated, may hold values from 0.5 to 1.5
- shortcut_shift: float32 [512], replicated, may hold values from -1.8 to 1.8
- second_kernel: bfloat16 [512, 512], replicated, may hold values from -0.25 to 0.25
- second_gain: float32 [512], replicated, may hold values from 0.5 to 1.5
- second_shift: float32 [512], replicated, may hold values from -1.8 to 1.8
- spatial_kernel: bfloat16 [3, 3, 64, 512], replicated, may hold values from -0.25 to 0.25
- spatial_gain: float32 [512], replicated, may hold values from 0.5 to 1.5
- spatial_shift: float32 [512], replicated, may hold values from -1.8 to 1.8
- reduce_weight: bfloat16 [512, 128], replicated, may hold values from -0.5 to 0.5
- reduce_bias: float32 [128], replicated, may hold values from -3 to 3
- expand_weight: bfloat16 [128, 512], replicated, may hold values from -0.5 to 0.5
- expand_bias: float32 [512], replicated, may hold values from -3 to 3
- final_kernel: bfloat16 [512, 512], replicated, may hold values from -0.25 to 0.25
- final_gain: float32 [512], replicated, may hold values from 0.5 to 1.5
- final_shift: float32 [512], replicated, may hold values from -1.8 to 1.8
- cotangent: bfloat16 [512, 20, 20, 512], P('img', 'ha', 'wa'), may hold values from -6 to 6
Outputs:
- activations: bfloat16 [512, 20, 20, 512], P('img', 'ha', 'wa')
- images_grad: bfloat16 [512, 40, 40, 192], P('img', 'ha', 'wa')
- grad_entry_kernel: float32 [192, 512], replicated
- grad_entry_gain: float32 [512], replicated
- grad_entry_shift: float32 [512], replicated
- grad_group_kernel: float32 [3, 3, 64, 512], replicated
- grad_group_gain: float32 [512], replicated
- grad_group_shift: float32 [512], replicated
- grad_squeeze_weight: float32 [512, 48], replicated
- grad_squeeze_bias: float32 [48], replicated
- grad_excite_weight: float32 [48, 512], replicated
- grad_excite_bias: float32 [512], replicated
- grad_output_kernel: float32 [512, 512], replicated
- grad_output_gain: float32 [512], replicated
- grad_output_shift: float32 [512], replicated
- grad_shortcut_kernel: float32 [192, 512], replicated
- grad_shortcut_gain: float32 [512], replicated
- grad_shortcut_shift: float32 [512], replicated
- grad_second_kernel: float32 [512, 512], replicated
- grad_second_gain: float32 [512], replicated
- grad_second_shift: float32 [512], replicated
- grad_spatial_kernel: float32 [3, 3, 64, 512], replicated
- grad_spatial_gain: float32 [512], replicated
- grad_spatial_shift: float32 [512], replicated
- grad_reduce_weight: float32 [512, 128], replicated
- grad_reduce_bias: float32 [128], replicated
- grad_expand_weight: float32 [128, 512], replicated
- grad_expand_bias: float32 [512], replicated
- grad_final_kernel: float32 [512, 512], replicated
- grad_final_gain: float32 [512], replicated
- grad_final_shift: float32 [512], replicated
Inputs may be any that keep to these rules, and one draw needn't show every extreme that they name: `classes`: every index of img holds a live image of class 2. `image_counts`: live images fill the first slots of an index; one index holds 64 images and another 64 // 2.
All inputs are finite; a program needn't handle non-finite values.
Results may differ from a plain program's by a relative error of at most 0.028.
Values may be sent and summed in bfloat16 or wider, within the bound.
A program may use at most 384 MiB of HBM per device.

v0:
```python
import jax
import jax.numpy as jnp
from jax import lax
from jax.sharding import PartitionSpec as P

EPS = 1e-05
HIGH = lax.Precision.HIGHEST
FORWARD = "shwgi,igo->shwgo"
BACKWARD = "shwgo,igo->shwgi"


def with_halo(cells, sides, width):
    for axis, dim in sides:
        count = lax.axis_size(axis)
        ends = count - 1
        head = lax.slice_in_dim(cells, 0, width, axis=dim)
        tail = lax.slice_in_dim(cells, cells.shape[dim] - width, cells.shape[dim], axis=dim)
        cells = jnp.concatenate(
            [
                lax.ppermute(tail, axis, [(i, (i + 1) % count) for i in range(ends)]),
                cells,
                lax.ppermute(head, axis, [((i + 1) % count, i) for i in range(ends)]),
            ],
            axis=dim,
        )
    return cells


def shifted(array, axis, by):
    length = lax.axis_size(axis)
    pairs = [(i, i + by) for i in range(length) if 0 <= i + by < length]
    return lax.ppermute(array, axis, pairs)


def slope(field):
    logistic = jax.nn.sigmoid(field)
    return logistic * (1.0 + field * (1.0 - logistic))


def inside(living, side_cells, row_pos, col_pos):
    rows_ok = (row_pos[None, :] < side_cells[:, None]).astype(jnp.float32)
    cols_ok = (col_pos[None, :] < side_cells[:, None]).astype(jnp.float32)
    return (living[:, None, None] * rows_ok[:, :, None] * cols_ok[:, None, :])[..., None]


def tile_masks(classes, image_counts, slot_count, rows_in, cols_in):
    positions = jnp.arange(classes.shape[0], dtype=jnp.int32)
    occupied = (positions % slot_count < jnp.repeat(image_counts, slot_count)).astype(jnp.float32)
    all_sides = 10 + 4 * classes
    cells_out = jnp.sum(occupied * (all_sides * all_sides).astype(jnp.float32))
    cells_in = 4.0 * cells_out
    offset = lax.axis_index("img") * slot_count
    side_cells = lax.dynamic_slice_in_dim(all_sides, offset, slot_count)
    living = lax.dynamic_slice_in_dim(occupied, offset, slot_count)
    row_in = lax.axis_index("ha") * rows_in + jnp.arange(rows_in, dtype=jnp.int32)
    col_in = lax.axis_index("wa") * cols_in + jnp.arange(cols_in, dtype=jnp.int32)
    row_out = lax.axis_index("ha") * (rows_in // 2) + jnp.arange(rows_in // 2, dtype=jnp.int32)
    col_out = lax.axis_index("wa") * (cols_in // 2) + jnp.arange(cols_in // 2, dtype=jnp.int32)
    mask_in = inside(living, 2 * side_cells, row_in, col_in)
    mask_out = inside(living, side_cells, row_out, col_out)
    pixels = (side_cells * side_cells).astype(jnp.float32)
    return (mask_in, mask_out, pixels, cells_in, cells_out)


def moments(fields, region, cell_count):
    totals = jnp.stack([jnp.sum(field * region, axis=(0, 1, 2)) for field in fields])
    squares = jnp.stack([jnp.sum(field * field * region, axis=(0, 1, 2)) for field in fields])
    totals, squares = lax.psum((totals, squares), ("ha", "wa", "img"))
    center = totals / cell_count
    factor = lax.rsqrt(squares / cell_count - center * center + EPS)
    return (center, factor)


def moment_grads(upstreams, normals):
    shift_sums = jnp.stack([jnp.sum(upstream, axis=(0, 1, 2)) for upstream in upstreams])
    gain_sums = jnp.stack(
        [jnp.sum(upstream * normal, axis=(0, 1, 2)) for upstream, normal in zip(upstreams, normals)]
    )
    return lax.psum((shift_sums, gain_sums), ("ha", "wa", "img"))


def norm_back(upstream, normal, gain_values, factor, shift_sum, gain_sum, region, cell_count):
    return (
        gain_values * factor * (upstream - region * (shift_sum + normal * gain_sum) / cell_count)
    ).astype(jnp.bfloat16)


def image_sums(field):
    return lax.psum(jnp.sum(field, axis=(1, 2)).astype(jnp.bfloat16), ("ha", "wa")).astype(
        jnp.float32
    )


def project(field, matrix):
    return jnp.einsum("shwc,cd->shwd", field, matrix, preferred_element_type=jnp.float32)


def back_project(gradient, matrix):
    return jnp.einsum("shwd,cd->shwc", gradient, matrix, preferred_element_type=jnp.float32)


def contract(left_side, right_side):
    return jnp.einsum("shwc,shwd->cd", left_side, right_side, preferred_element_type=jnp.float32)


def taps(field, kernel, stride, rows_out, cols_out, formula):
    result = None
    for tap_row in range(3):
        for tap_col in range(3):
            window = field[
                :,
                tap_row : tap_row + stride * (rows_out - 1) + 1 : stride,
                tap_col : tap_col + stride * (cols_out - 1) + 1 : stride,
            ]
            product = jnp.einsum(
                formula, window, kernel[tap_row, tap_col], preferred_element_type=jnp.float32
            )
            result = product if result is None else result + product
    return result


def kernel_grad(field, gradient, stride, rows_out, cols_out):
    pieces = []
    for tap_row in range(3):
        for tap_col in range(3):
            window = field[
                :,
                tap_row : tap_row + stride * (rows_out - 1) + 1 : stride,
                tap_col : tap_col + stride * (cols_out - 1) + 1 : stride,
            ]
            pieces.append(
                jnp.einsum("shwgi,shwgo->igo", window, gradient, preferred_element_type=jnp.float32)
            )
    stacked = jnp.stack(pieces)
    return stacked.reshape((3, 3) + stacked.shape[1:2] + (-1,))


def spread(gradient, kernel, rows_out, cols_out):
    extent = gradient.shape
    canvas = jnp.zeros(
        (extent[0], 2 * rows_out + 1, 2 * cols_out + 1, extent[3], kernel.shape[2]), jnp.float32
    )
    for tap_row in range(3):
        for tap_col in range(3):
            product = jnp.einsum(
                BACKWARD, gradient, kernel[tap_row, tap_col], preferred_element_type=jnp.float32
            )
            canvas = canvas.at[
                :,
                tap_row : tap_row + 2 * rows_out - 1 : 2,
                tap_col : tap_col + 2 * cols_out - 1 : 2,
            ].add(product)
    return canvas


def bordered(field):
    return with_halo(field, (("ha", 1), ("wa", 2)), 1)


def excite_forward(gated, pixels, down_weight, down_bias, upward, up_bias):
    pooled = image_sums(gated) / pixels[:, None]
    before = jnp.dot(pooled, down_weight, precision=HIGH) + down_bias
    hidden = jax.nn.silu(before)
    scaling = jax.nn.sigmoid(jnp.dot(hidden, upward, precision=HIGH) + up_bias)
    return (pooled, before, hidden, scaling)


def excite_backward(
    dexcited, gated, pooled, before, hidden, scaling, pixels, down_weight, upward, owner
):
    dscaling = image_sums(dexcited * gated)
    dlogit = dscaling * scaling * (1.0 - scaling)
    upward_grad = jnp.dot(hidden.T, dlogit, precision=HIGH) * owner
    upward_bias_grad = jnp.sum(dlogit, axis=0) * owner
    dhidden = jnp.dot(dlogit, upward.T, precision=HIGH)
    dbefore = dhidden * slope(before)
    down_grad = jnp.dot(pooled.T, dbefore, precision=HIGH) * owner
    down_bias_grad = jnp.sum(dbefore, axis=0) * owner
    dpooled = jnp.dot(dbefore, down_weight.T, precision=HIGH)
    dgated = dexcited * scaling[:, None, None, :] + (dpooled / pixels[:, None])[:, None, None, :]
    return (dgated, down_grad, down_bias_grad, upward_grad, upward_bias_grad)


def body(
    images,
    classes,
    image_counts,
    entry_kernel,
    entry_gain,
    entry_shift,
    group_kernel,
    group_gain,
    group_shift,
    squeeze_weight,
    squeeze_bias,
    excite_weight,
    excite_bias,
    output_kernel,
    output_gain,
    output_shift,
    shortcut_kernel,
    shortcut_gain,
    shortcut_shift,
    second_kernel,
    second_gain,
    second_shift,
    spatial_kernel,
    spatial_gain,
    spatial_shift,
    reduce_weight,
    reduce_bias,
    expand_weight,
    expand_bias,
    final_kernel,
    final_gain,
    final_shift,
    cotangent,
):
    slot_count, rows_in, cols_in, inputs = images.shape
    rows_out, cols_out = (rows_in // 2, cols_in // 2)
    channels = entry_kernel.shape[1]
    group_width = group_kernel.shape[2]
    group_count = channels // group_width
    mask_in, mask_out, pixels, cells_in, cells_out = tile_masks(
        classes, image_counts, slot_count, rows_in, cols_in
    )
    owner = jnp.logical_and(lax.axis_index("ha") == 0, lax.axis_index("wa") == 0).astype(
        jnp.float32
    )
    squeeze_float = squeeze_weight.astype(jnp.float32)
    excite_float = excite_weight.astype(jnp.float32)
    reduce_float = reduce_weight.astype(jnp.float32)
    expand_float = expand_weight.astype(jnp.float32)
    start = images * mask_in.astype(jnp.bfloat16)
    entry = project(start, entry_kernel)
    center_a, factor_a = moments([entry], mask_in, cells_in)
    normal_a = (entry - center_a[0]) * factor_a[0]
    before_a = normal_a * entry_gain + entry_shift
    active = (jax.nn.silu(before_a) * mask_in).astype(jnp.bfloat16)
    upper_rim = shifted(active[:, -1:], "ha", 1)
    with_rows = jnp.concatenate([upper_rim, active], axis=1)
    left_rim = shifted(with_rows[:, :, -1:], "wa", 1)
    framed = jnp.concatenate([left_rim, with_rows], axis=2)
    framed_groups = framed.reshape(slot_count, rows_in + 1, cols_in + 1, group_count, group_width)
    kernel_one = group_kernel.reshape(3, 3, group_width, group_count, group_width)
    middle = taps(framed_groups, kernel_one, 2, rows_out, cols_out, FORWARD).reshape(
        slot_count, rows_out, cols_out, channels
    )
    center_b, factor_b = moments([middle], mask_out, cells_out)
    normal_b = (middle - center_b[0]) * factor_b[0]
    before_b = normal_b * group_gain + group_shift
    gated = jax.nn.silu(before_b) * mask_out
    pooled_one, hidden_pre_one, hidden_one, scaling_one = excite_forward(
        gated, pixels, squeeze_float, squeeze_bias, excite_float, excite_bias
    )
    excited = (gated * scaling_one[:, None, None, :]).astype(jnp.bfloat16)
    branch = project(excited, output_kernel)
    strided = start[:, ::2, ::2]
    bypass = project(strided, shortcut_kernel)
    center_c, factor_c = moments([branch, bypass], mask_out, cells_out)
    normal_c = (branch - center_c[0]) * factor_c[0]
    normal_s = (bypass - center_c[1]) * factor_c[1]
    total_one = normal_c * output_gain + output_shift + normal_s * shortcut_gain + shortcut_shift
    middle_out = (jax.nn.silu(total_one) * mask_out).astype(jnp.bfloat16)
    second = project(middle_out, second_kernel)
    center_d, factor_d = moments([second], mask_out, cells_out)
    normal_d = (second - center_d[0]) * factor_d[0]
    before_d = normal_d * second_gain + second_shift
    active_two = (jax.nn.silu(before_d) * mask_out).astype(jnp.bfloat16)
    framed_two = bordered(active_two).reshape(
        slot_count, rows_out + 2, cols_out + 2, group_count, group_width
    )
    kernel_two = spatial_kernel.reshape(3, 3, group_width, group_count, group_width)
    spatial = taps(framed_two, kernel_two, 1, rows_out, cols_out, FORWARD).reshape(
        slot_count, rows_out, cols_out, channels
    )
    center_e, factor_e = moments([spatial], mask_out, cells_out)
    normal_e = (spatial - center_e[0]) * factor_e[0]
    before_e = normal_e * spatial_gain + spatial_shift
    gated_two = jax.nn.silu(before_e) * mask_out
    pooled_two, hidden_pre_two, hidden_two, scaling_two = excite_forward(
        gated_two, pixels, reduce_float, reduce_bias, expand_float, expand_bias
    )
    excited_two = (gated_two * scaling_two[:, None, None, :]).astype(jnp.bfloat16)
    final = project(excited_two, final_kernel)
    center_f, factor_f = moments([final], mask_out, cells_out)
    normal_f = (final - center_f[0]) * factor_f[0]
    total_two = normal_f * final_gain + final_shift + middle_out.astype(jnp.float32)
    activations = (jax.nn.silu(total_two) * mask_out).astype(jnp.bfloat16)
    upstream_f = cotangent.astype(jnp.float32) * mask_out * slope(total_two)
    shift_f, gain_f = moment_grads([upstream_f], [normal_f])
    dfinal = norm_back(
        upstream_f, normal_f, final_gain, factor_f[0], shift_f[0], gain_f[0], mask_out, cells_out
    )
    final_grad = contract(excited_two, dfinal)
    dexcited_two = back_project(dfinal, final_kernel)
    dgated_two, reduce_grad, reduce_bias_grad, expand_grad, expand_bias_grad = excite_backward(
        dexcited_two,
        gated_two,
        pooled_two,
        hidden_pre_two,
        hidden_two,
        scaling_two,
        pixels,
        reduce_float,
        expand_float,
        owner,
    )
    upstream_e = dgated_two * mask_out * slope(before_e)
    shift_e, gain_e = moment_grads([upstream_e], [normal_e])
    dspatial = norm_back(
        upstream_e, normal_e, spatial_gain, factor_e[0], shift_e[0], gain_e[0], mask_out, cells_out
    )
    dspatial_groups = dspatial.reshape(slot_count, rows_out, cols_out, group_count, group_width)
    spatial_grad = kernel_grad(framed_two, dspatial_groups, 1, rows_out, cols_out)
    dframed_two = bordered(dspatial).reshape(
        slot_count, rows_out + 2, cols_out + 2, group_count, group_width
    )
    dactive_two = taps(
        dframed_two, kernel_two[::-1, ::-1], 1, rows_out, cols_out, BACKWARD
    ).reshape(slot_count, rows_out, cols_out, channels)
    upstream_d = dactive_two * mask_out * slope(before_d)
    shift_d, gain_d = moment_grads([upstream_d], [normal_d])
    dsecond = norm_back(
        upstream_d, normal_d, second_gain, factor_d[0], shift_d[0], gain_d[0], mask_out, cells_out
    )
    second_grad = contract(middle_out, dsecond)
    dmiddle_out = upstream_f + back_project(dsecond, second_kernel)
    upstream_c = dmiddle_out * mask_out * slope(total_one)
    shift_c, gain_c = moment_grads([upstream_c, upstream_c], [normal_c, normal_s])
    dbranch = norm_back(
        upstream_c, normal_c, output_gain, factor_c[0], shift_c[0], gain_c[0], mask_out, cells_out
    )
    dbypass = norm_back(
        upstream_c, normal_s, shortcut_gain, factor_c[1], shift_c[1], gain_c[1], mask_out, cells_out
    )
    output_grad = contract(excited, dbranch)
    shortcut_grad = contract(strided, dbypass)
    dstrided = back_project(dbypass, shortcut_kernel)
    dexcited = back_project(dbranch, output_kernel)
    dgated, squeeze_grad, squeeze_bias_grad, excite_grad, excite_bias_grad = excite_backward(
        dexcited,
        gated,
        pooled_one,
        hidden_pre_one,
        hidden_one,
        scaling_one,
        pixels,
        squeeze_float,
        excite_float,
        owner,
    )
    upstream_b = dgated * mask_out * slope(before_b)
    shift_b, gain_b = moment_grads([upstream_b], [normal_b])
    dmiddle = norm_back(
        upstream_b, normal_b, group_gain, factor_b[0], shift_b[0], gain_b[0], mask_out, cells_out
    )
    dmiddle_groups = dmiddle.reshape(slot_count, rows_out, cols_out, group_count, group_width)
    group_grad = kernel_grad(framed_groups, dmiddle_groups, 2, rows_out, cols_out)
    dframed = spread(dmiddle_groups, kernel_one, rows_out, cols_out).reshape(
        slot_count, rows_in + 1, cols_in + 1, channels
    )
    from_right = shifted(dframed[:, :, :1].astype(jnp.bfloat16), "wa", -1).astype(jnp.float32)
    dwith_rows = dframed[:, :, 1:]
    dwith_rows = dwith_rows.at[:, :, -1:].add(from_right)
    from_below = shifted(dwith_rows[:, :1].astype(jnp.bfloat16), "ha", -1).astype(jnp.float32)
    dactive = dwith_rows[:, 1:].at[:, -1:].add(from_below)
    upstream_a = dactive * mask_in * slope(before_a)
    shift_a, gain_a = moment_grads([upstream_a], [normal_a])
    dentry = norm_back(
        upstream_a, normal_a, entry_gain, factor_a[0], shift_a[0], gain_a[0], mask_in, cells_in
    )
    entry_grad = contract(start, dentry)
    dstart = back_project(dentry, entry_kernel)
    dstart = dstart.at[:, ::2, ::2].add(dstrided)
    images_grad = (dstart * mask_in).astype(jnp.bfloat16)
    (
        entry_grad,
        group_grad,
        squeeze_grad,
        squeeze_bias_grad,
        excite_grad,
        excite_bias_grad,
        output_grad,
        shortcut_grad,
        second_grad,
        spatial_grad,
        reduce_grad,
        reduce_bias_grad,
        expand_grad,
        expand_bias_grad,
        final_grad,
    ) = lax.psum(
        (
            entry_grad,
            group_grad,
            squeeze_grad,
            squeeze_bias_grad,
            excite_grad,
            excite_bias_grad,
            output_grad,
            shortcut_grad,
            second_grad,
            spatial_grad,
            reduce_grad,
            reduce_bias_grad,
            expand_grad,
            expand_bias_grad,
            final_grad,
        ),
        ("ha", "wa", "img"),
    )
    return (
        activations,
        images_grad,
        entry_grad,
        gain_a[0],
        shift_a[0],
        group_grad,
        gain_b[0],
        shift_b[0],
        squeeze_grad,
        squeeze_bias_grad,
        excite_grad,
        excite_bias_grad,
        output_grad,
        gain_c[0],
        shift_c[0],
        shortcut_grad,
        gain_c[1],
        shift_c[1],
        second_grad,
        gain_d[0],
        shift_d[0],
        spatial_grad,
        gain_e[0],
        shift_e[0],
        reduce_grad,
        reduce_bias_grad,
        expand_grad,
        expand_bias_grad,
        final_grad,
        gain_f[0],
        shift_f[0],
    )


def solution(mesh):
    placed = (
        P("img", "ha", "wa", None),
        P(),
        P(),
        P(),
        P(),
        P(),
        P(),
        P(),
        P(),
        P(),
        P(),
        P(),
        P(),
        P(),
        P(),
        P(),
        P(),
        P(),
        P(),
        P(),
        P(),
        P(),
        P(),
        P(),
        P(),
        P(),
        P(),
        P(),
        P(),
        P(),
        P(),
        P(),
        P("img", "ha", "wa", None),
    )
    return jax.shard_map(
        body,
        mesh=mesh,
        in_specs=placed,
        out_specs=(
            P("img", "ha", "wa", None),
            P("img", "ha", "wa", None),
            P(),
            P(),
            P(),
            P(),
            P(),
            P(),
            P(),
            P(),
            P(),
            P(),
            P(),
            P(),
            P(),
            P(),
            P(),
            P(),
            P(),
            P(),
            P(),
            P(),
            P(),
            P(),
            P(),
            P(),
            P(),
            P(),
            P(),
            P(),
            P(),
        ),
        check_vma=False,
    )
```

profile of v0, /device:TPU:0, one launch (start us, length us, event | category | flops | bytes accessed | tf_op | source)
XLA Modules:
  0.0 2236.2 jit_solution(16024285397774809083)
XLA Ops:
  20.7 68.1 %all-reduce.11 = (f32[1,512]{1,0:T(1,128)S(1)}, f32[1,512]{1,0:T(1,128)S(1)}) all-reduce(f32[1,512]{1,0:T(1,128)S(1)} %bitcast.666, f32[1,512]{1,0:T(1,128)S(1)} %bitcast.665), channel_id=1, replica_groups=mesh['ha'=4,'wa'=4,'img'=8] {'ha','wa','img'}, use_global_device_ids=true, to_apply=%region_1.2 | all-reduce | flops 1024 | bytes 8192 | tf_op jit(solution)/shard_map/psum | solution.py:68
  125.3 9.7 collective-permute-done.1
  139.0 20.3 reshape.413
  159.3 23.5 %fusion.288 = (bf16[64,5,5,8,64]{4,3,0,2,1:T(8,128)(2,1)}, bf16[64,5,5,8,64]{4,3,0,2,1:T(8,128)(2,1)}, bf16[64,5,5,8,64]{4,3,0,2,1:T(8,128)(2,1)}, bf16[64,5,5,8...) fusion(bf16[64,11,11,8,64]{4,3,0,2,1:T(8,128)(2,1)} %reshape.413), kind=kLoop, calls=%fused_computation.401 | loop fusion | bytes 29491200 | tf_op jit(solution)/shard_map/slice | solution.py:110
  208.5 15.8 multiply_reduce_fusion.7
  224.4 67.0 %all-reduce.10 = (f32[1,512]{1,0:T(1,128)S(1)}, f32[1,512]{1,0:T(1,128)S(1)}) all-reduce(f32[1,512]{1,0:T(1,128)S(1)} %stack.156, f32[1,512]{1,0:T(1,128)S(1)} %stack.157), channel_id=1, replica_groups=mesh['ha'=4,'wa'=4,'img'=8] {'ha','wa','img'}, use_global_device_ids=true, to_apply=%region_6.7 | all-reduce | flops 1024 | bytes 8192 | tf_op jit(solution)/shard_map/psum | solution.py:68
  300.8 11.3 copy.235
  318.7 58.7 %all-reduce.19.cloned.1.call-done = bf16[64,512]{1,0:T(8,128)(2,1)} async-done(((bf16[64,512]{1,0:T(8,128)(2,1)}), bf16[64,512]{1,0:T(8,128)(2,1)}) %all-reduce.19.cloned.1.call-update) | async-done | bytes 65552 | tf_op jit(solution)/shard_map/psum | solution.py:89
  384.6 64.9 %all-reduce.9 = (f32[2,512]{1,0:T(2,128)S(1)}, f32[2,512]{1,0:T(2,128)S(1)}) all-reduce(f32[2,512]{1,0:T(2,128)S(1)} %get-tuple-element.250, f32[2,512]{1,0:T(2,128)S(1)} %get-tuple-element.251), channel_id=1, replica_groups=mesh['ha'=4,'wa'=4,'img'=8] {'ha','wa','img'}, use_global_device_ids=true, to_apply=%region_13.14 | all-reduce | flops 2048 | bytes 16384 | tf_op jit(solution)/shard_map/psum | solution.py:68
  457.0 61.9 %all-reduce.8 = (f32[1,512]{1,0:T(1,128)S(1)}, f32[1,512]{1,0:T(1,128)S(1)}) all-reduce(f32[1,512]{1,0:T(1,128)S(1)} %bitcast.668, f32[1,512]{1,0:T(1,128)S(1)} %bitcast.667), channel_id=1, replica_groups=mesh['ha'=4,'wa'=4,'img'=8] {'ha','wa','img'}, use_global_device_ids=true, to_apply=%region_18.19 | all-reduce | flops 1024 | bytes 8192 | tf_op jit(solution)/shard_map/psum | solution.py:68
  553.9 9.0 reshape.416
  562.9 24.4 %fusion.290 = (bf16[64,5,5,8,64]{4,3,0,2,1:T(8,128)(2,1)}, bf16[64,5,5,8,64]{4,3,0,2,1:T(8,128)(2,1)}, bf16[64,5,5,8,64]{4,3,0,2,1:T(8,128)(2,1)}, bf16[64,5,5,8...) fusion(bf16[64,7,7,8,64]{4,3,0,2,1:T(8,128)(2,1)} %reshape.416), kind=kLoop, calls=%fused_computation.403 | loop fusion | bytes 29491200 | tf_op jit(solution)/shard_map/slice | solution.py:110
  612.9 15.9 multiply_reduce_fusion.4
  628.9 62.3 %all-reduce.7 = (f32[1,512]{1,0:T(1,128)S(1)}, f32[1,512]{1,0:T(1,128)S(1)}) all-reduce(f32[1,512]{1,0:T(1,128)S(1)} %stack.166, f32[1,512]{1,0:T(1,128)S(1)} %stack.167), channel_id=1, replica_groups=mesh['ha'=4,'wa'=4,'img'=8] {'ha','wa','img'}, use_global_device_ids=true, to_apply=%region_22.23 | all-reduce | flops 1024 | bytes 8192 | tf_op jit(solution)/shard_map/psum | solution.py:68
  707.4 11.3 copy.255
  725.5 52.2 %all-reduce.21.cloned.1.call-done = bf16[64,512]{1,0:T(8,128)(2,1)} async-done(((bf16[64,512]{1,0:T(8,128)(2,1)}), bf16[64,512]{1,0:T(8,128)(2,1)}) %all-reduce.21.cloned.1.call-update) | async-done | bytes 65552 | tf_op jit(solution)/shard_map/psum | solution.py:89
  784.8 64.6 %all-reduce.6 = (f32[1,512]{1,0:T(1,128)S(1)}, f32[1,512]{1,0:T(1,128)S(1)}) all-reduce(f32[1,512]{1,0:T(1,128)S(1)} %bitcast.670, f32[1,512]{1,0:T(1,128)S(1)} %bitcast.669), channel_id=1, replica_groups=mesh['ha'=4,'wa'=4,'img'=8] {'ha','wa','img'}, use_global_device_ids=true, to_apply=%region_28.29 | all-reduce | flops 1024 | bytes 8192 | tf_op jit(solution)/shard_map/psum | solution.py:68
  855.6 61.9 %all-reduce.5 = (f32[512]{0:T(512)S(1)}, f32[512]{0:T(512)S(1)}) all-reduce(f32[512]{0:T(512)S(1)} %get-tuple-element.81, f32[512]{0:T(512)S(1)} %get-tuple-element.80), channel_id=1, replica_groups=mesh['ha'=4,'wa'=4,'img'=8] {'ha','wa','img'}, use_global_device_ids=true, to_apply=%region_34.35 | all-reduce | flops 1024 | bytes 8192 | tf_op jit(solution)/shard_map/psum | solution.py:79
  931.4 73.4 %all-reduce.23.cloned.1.call-done = bf16[64,512]{1,0:T(8,128)(2,1)} async-done(((bf16[64,512]{1,0:T(8,128)(2,1)}), bf16[64,512]{1,0:T(8,128)(2,1)}) %all-reduce.23.cloned.1.call-update) | async-done | bytes 65552 | tf_op jit(solution)/shard_map/psum | solution.py:89
  1011.4 64.6 %all-reduce.4 = (f32[512]{0:T(512)S(1)}, f32[512]{0:T(512)S(1)}) all-reduce(f32[512]{0:T(512)S(1)} %get-tuple-element.79, f32[512]{0:T(512)S(1)} %get-tuple-element.78), channel_id=1, replica_groups=mesh['ha'=4,'wa'=4,'img'=8] {'ha','wa','img'}, use_global_device_ids=true, to_apply=%region_40.41 | all-reduce | flops 1024 | bytes 8192 | tf_op jit(solution)/shard_map/psum | solution.py:79
  1143.8 9.0 reshape.419
  1152.8 24.2 %fusion.289 = (bf16[64,5,5,8,64]{4,3,0,2,1:T(8,128)(2,1)}, bf16[64,5,5,8,64]{4,3,0,2,1:T(8,128)(2,1)}, bf16[64,5,5,8,64]{4,3,0,2,1:T(8,128)(2,1)}, bf16[64,5,5,8...) fusion(bf16[64,7,7,8,64]{4,3,0,2,1:T(8,128)(2,1)} %reshape.419), kind=kLoop, calls=%fused_computation.402 | loop fusion | bytes 29491200 | tf_op jit(solution)/shard_map/slice | solution.py:110
  1202.6 14.6 add_bitcast_fusion
  1217.2 11.3 copy.266
  1240.1 62.6 %all-reduce.3 = (f32[512]{0:T(512)S(1)}, f32[512]{0:T(512)S(1)}) all-reduce(f32[512]{0:T(512)S(1)} %get-tuple-element.77, f32[512]{0:T(512)S(1)} %get-tuple-element.76), channel_id=1, replica_groups=mesh['ha'=4,'wa'=4,'img'=8] {'ha','wa','img'}, use_global_device_ids=true, to_apply=%region_44.45 | all-reduce | flops 1024 | bytes 8192 | tf_op jit(solution)/shard_map/psum | solution.py:79
  1314.9 62.6 %all-reduce.2 = (f32[2,512]{1,0:T(2,128)S(1)}, f32[2,512]{1,0:T(2,128)S(1)}) all-reduce(f32[2,512]{1,0:T(2,128)S(1)} %pad_maximum_fusion.12, f32[2,512]{1,0:T(2,128)S(1)} %pad_maximum_fusion.11), channel_id=1, replica_groups=mesh['ha'=4,'wa'=4,'img'=8] {'ha','wa','img'}, use_global_device_ids=true, to_apply=%region_49.50 | all-reduce | flops 2048 | bytes 16384 | tf_op jit(solution)/shard_map/psum | solution.py:79
  1395.1 75.8 %all-reduce.25.cloned.1.call-done = bf16[64,512]{1,0:T(8,128)(2,1)} async-done(((bf16[64,512]{1,0:T(8,128)(2,1)}), bf16[64,512]{1,0:T(8,128)(2,1)}) %all-reduce.25.cloned.1.call-update) | async-done | bytes 65552 | tf_op jit(solution)/shard_map/psum | solution.py:89
  1478.2 64.6 %all-reduce.1 = (f32[512]{0:T(512)S(1)}, f32[512]{0:T(512)S(1)}) all-reduce(f32[512]{0:T(512)S(1)} %get-tuple-element.72, f32[512]{0:T(512)S(1)} %get-tuple-element.71), channel_id=1, replica_groups=mesh['ha'=4,'wa'=4,'img'=8] {'ha','wa','img'}, use_global_device_ids=true, to_apply=%region_55.56 | all-reduce | flops 1024 | bytes 8192 | tf_op jit(solution)/shard_map/psum | solution.py:79
  1620.1 9.0 copy.276
  1654.9 8.8 copy.284
  1663.7 10.4 broadcast_in_dim.41
  1674.2 18.2 scatter_fusion
  1692.3 18.1 scatter_fusion.1
  1710.4 18.1 scatter_fusion.2
  1728.5 18.1 scatter_fusion.3
  1746.7 18.0 scatter_fusion.4
  1764.7 18.1 scatter_fusion.5
  1782.8 18.2 scatter_fusion.6
  1801.0 18.1 scatter_fusion.7
  1819.1 18.3 scatter_fusion.8
  1837.4 30.8 %reshape.542 = f32[64,11,11,512]{3,2,1,0:T(8,128)} reshape(f32[64,11,11,8,64]{4,3,2,1,0:T(8,128)} %scatter_fusion.8) | data formatting | bytes 31719424 | tf_op jit(solution)/shard_map/reshape | solution.py:360
  1868.2 18.0 slice.454
  1918.2 16.2 copy.398
  1943.2 12.4 slice.457
  1960.6 15.5 fusion.277
  1976.1 62.9 %all-reduce = (f32[512]{0:T(512)S(1)}, f32[512]{0:T(512)S(1)}, f32[48]{0:T(128)}, f32[512]{0:T(512)}, f32[128]{0:T(128)}, /*index=5*/f32[512]{0:T(512)}) all-reduce(f32[512]{0:T(512)S(1)} %get-tuple-element.58, f32[512]{0:T(512)S(1)} %get-tuple-element.57, ...), channel_id=1, replica_groups=mesh['ha'=4,'wa'=4,'img'=8] {'ha','wa','img'}, use_global_device_ids=true, to_apply=%region_68.69 | all-reduce | flops 2224 | bytes 17792 | tf_op jit(solution)/shard_map/psum | solution.py:79
  2039.1 10.0 multiply_convert_fusion
  2075.8 140.8 %all-reduce.27.cloned.1.call-done = (f32[192,512]{1,0:T(8,128)}, f32[3,3,64,512]{3,2,1,0:T(8,128)}, f32[512,48]{0,1:T(8,128)}, f32[48,512]{1,0:T(8,128)}, f32[51...) async-done(((f32[192,512]{1,0:T(8,128)}, ...) | async-done | bytes 7012368 | tf_op jit(solution)/shard_map/psum | solution.py:393
  (713 shorter events, 555.5 us)
Async XLA Ops:
  7.2 371.6 %copy-start = (bf16[512,512]{1,0:T(8,128)(2,1)S(1)}, bf16[512,512]{1,0:T(8,128)(2,1)}, u32[]{:S(2)}) copy-start(bf16[512,512]{1,0:T(8,128)(2,1)} %param.50) | copy-start | bytes 1572868
  7.2 370.1 %all-reduce.19.cloned.1.call-start = ((), (), s32[]{:S(2)}) async-start(), calls=%async_computation | async-start | bytes 131072 | tf_op jit(solution)/shard_map/psum | solution.py:89
  11.9 77.5 %copy-start.69 = (f32[64,10,10]{0,2,1:T(8,128)}, f32[64,10,10]{0,2,1:T(8,128)S(1)}, u32[]{:S(2)}) copy-start(f32[64,10,10]{0,2,1:T(8,128)S(1)} %get-tuple-element.204) | copy-start | bytes 76804
  14.4 75.0 %copy-start.149 = (f32[512]{0:T(512)S(1)}, f32[512]{0:T(512)}, u32[]{:S(2)}) copy-start(f32[512]{0:T(512)} %param.41) | copy-start | bytes 6148
  14.4 75.0 %copy-start.172 = (f32[512]{0:T(512)S(1)}, f32[512]{0:T(512)}, u32[]{:S(2)}) copy-start(f32[512]{0:T(512)} %param.42) | copy-start | bytes 6148
  100.7 15.9 collective-permute-start
  117.9 17.1 collective-permute-start.1
  121.6 65.4 %copy-start.86 = (bf16[1,1,64,8,64]{4,3,2,1,0:T(8,128)(2,1)}, bf16[1,1,64,8,64]{4,3,2,1,0:T(8,128)(2,1)S(1)}, u32[]{:S(2)}) copy-start(bf16[1,1,64,8,64]{4,3,2,1,0:T(8,128)(2,1)S(1)} %get-tuple-element.199) | copy-start | bytes 196612
  121.6 83.1 %copy-start.80 = (bf16[1,1,64,8,64]{4,3,2,1,0:T(8,128)(2,1)}, bf16[1,1,64,8,64]{4,3,2,1,0:T(8,128)(2,1)S(1)}, u32[]{:S(2)}) copy-start(bf16[1,1,64,8,64]{4,3,2,1,0:T(8,128)(2,1)S(1)} %get-tuple-element.196) | copy-start | bytes 196612
  293.1 85.7 %copy-start.131 = (f32[1,512]{1,0:T(1,128)}, f32[1,512]{1,0:T(1,128)S(1)}, u32[]{:S(2)}) copy-start(f32[1,512]{1,0:T(1,128)S(1)} %get-tuple-element.141) | copy-start | bytes 6148
  294.4 411.3 %copy-start.133 = (f32[1,512]{1,0:T(1,128)}, f32[1,512]{1,0:T(1,128)S(1)}, u32[]{:S(2)}) copy-start(f32[1,512]{1,0:T(1,128)S(1)} %get-tuple-element.143) | copy-start | bytes 6148
  300.2 477.5 %all-reduce.21.cloned.1.call-start = ((), (), s32[]{:S(2)}) async-start(), calls=%async_computation.1 | async-start | bytes 131072 | tf_op jit(solution)/shard_map/psum | solution.py:89
  312.0 65.3 %copy-start.205 = (bf16[512,48]{0,1:T(8,128)(2,1)S(1)}, bf16[512,48]{0,1:T(8,128)(2,1)}, u32[]{:S(2)}) copy-start(bf16[512,48]{0,1:T(8,128)(2,1)} %param.46) | copy-start | bytes 147460
  312.0 65.3 %copy-start.209 = (f32[48]{0:T(128)S(1)}, f32[48]{0:T(128)}, u32[]{:S(2)}) copy-start(f32[48]{0:T(128)} %param.47) | copy-start | bytes 580
  312.0 66.4 %copy-start.203 = (bf16[48,512]{1,0:T(8,128)(2,1)S(1)}, bf16[48,512]{1,0:T(8,128)(2,1)}, u32[]{:S(2)}) copy-start(bf16[48,512]{1,0:T(8,128)(2,1)} %param.48) | copy-start | bytes 147460
  312.0 66.4 %copy-start.207 = (f32[512]{0:T(512)S(1)}, f32[512]{0:T(512)}, u32[]{:S(2)}) copy-start(f32[512]{0:T(512)} %param.49) | copy-start | bytes 6148
  312.0 66.8 %copy-start.160 = (f32[512]{0:T(512)S(1)}, f32[512]{0:T(512)}, u32[]{:S(2)}) copy-start(f32[512]{0:T(512)} %param.45) | copy-start | bytes 6148
  378.8 71.3 %copy-start.157 = (f32[512]{0:T(512)S(1)}, f32[512]{0:T(512)}, u32[]{:S(2)}) copy-start(f32[512]{0:T(512)} %param.54) | copy-start | bytes 6148
  378.9 71.3 %copy-start.158 = (f32[512]{0:T(512)S(1)}, f32[512]{0:T(512)}, u32[]{:S(2)}) copy-start(f32[512]{0:T(512)} %param.51) | copy-start | bytes 6148
  378.9 71.3 %copy-start.175 = (f32[512]{0:T(512)S(1)}, f32[512]{0:T(512)}, u32[]{:S(2)}) copy-start(f32[512]{0:T(512)} %param.55) | copy-start | bytes 6148
  378.9 71.3 %copy-start.177 = (f32[512]{0:T(512)S(1)}, f32[512]{0:T(512)}, u32[]{:S(2)}) copy-start(f32[512]{0:T(512)} %param.52) | copy-start | bytes 6148
  454.1 65.5 %copy-start.140 = (f32[512]{0:T(512)S(1)}, f32[512]{0:T(512)}, u32[]{:S(2)}) copy-start(f32[512]{0:T(512)} %param.57) | copy-start | bytes 6148
  454.1 65.5 %copy-start.154 = (f32[512]{0:T(512)S(1)}, f32[512]{0:T(512)}, u32[]{:S(2)}) copy-start(f32[512]{0:T(512)} %param.58) | copy-start | bytes 6148
  522.3 10.3 collective-permute-start.2
  525.8 11.0 collective-permute-start.3
  536.9 10.9 collective-permute-start.4
  538.8 13.1 collective-permute-start.5
  612.9 81.0 %copy-start.152 = (f32[8,64]{1,0:T(8,128)S(1)}, f32[8,64]{1,0:T(8,128)}, u32[]{:S(2)}) copy-start(f32[8,64]{1,0:T(8,128)} %add.656) | copy-start | bytes 6148
  612.9 81.0 %copy-start.153 = (f32[8,64]{1,0:T(8,128)S(1)}, f32[8,64]{1,0:T(8,128)}, u32[]{:S(2)}) copy-start(f32[8,64]{1,0:T(8,128)} %mul.1044) | copy-start | bytes 6148
  699.5 305.3 %all-reduce.23.cloned.1.call-start = ((), (), s32[]{:S(2)}) async-start(), calls=%async_computation.2 | async-start | bytes 131072 | tf_op jit(solution)/shard_map/psum | solution.py:89
  779.1 70.9 %copy-start.171 = (f32[512]{0:T(512)S(1)}, f32[512]{0:T(512)}, u32[]{:S(2)}) copy-start(f32[512]{0:T(512)} %param.67) | copy-start | bytes 6148
  779.1 70.9 %copy-start.53 = (bf16[64,5,5,512]{3,0,2,1:T(8,128)(2,1)S(1)}, bf16[64,5,5,512]{3,0,2,1:T(8,128)(2,1)}, u32[]{:S(2)}) copy-start(bf16[64,5,5,512]{3,0,2,1:T(8,128)(2,1)} %copy-done.52) | copy-start | bytes 4915204
  779.1 70.9 %copy-start.191 = (f32[512]{0:T(512)S(1)}, f32[512]{0:T(512)}, u32[]{:S(2)}) copy-start(f32[512]{0:T(512)} %param.68) | copy-start | bytes 6148
  926.4 544.5 %all-reduce.25.cloned.1.call-start = ((), (), s32[]{:S(2)}) async-start(), calls=%async_computation.3 | async-start | bytes 131072 | tf_op jit(solution)/shard_map/psum | solution.py:89
  1111.7 8.6 collective-permute-start.6
  1113.2 11.4 collective-permute-start.7
  1125.5 11.3 collective-permute-start.8
  1128.4 12.6 collective-permute-start.9
  1307.9 69.6 %copy-start.164 = (f32[512]{0:T(512)S(1)}, f32[512]{0:T(512)}, u32[]{:S(2)}) copy-start(f32[512]{0:T(512)} %mul.1068) | copy-start | bytes 6148
  1307.9 69.6 %copy-start.165 = (f32[512]{0:T(512)S(1)}, f32[512]{0:T(512)}, u32[]{:S(2)}) copy-start(f32[512]{0:T(512)} %mul.1151) | copy-start | bytes 6148
  1390.5 80.5 %copy-start.138 = (f32[64,48]{0,1:T(8,128)S(1)}, f32[64,48]{0,1:T(8,128)}, u32[]{:S(2)}) copy-start(f32[64,48]{0,1:T(8,128)} %copy-done.137) | copy-start | bytes 36868
  1390.5 80.5 %copy-start.204 = (bf16[48,512]{1,0:T(8,128)(2,1)S(1)}, bf16[48,512]{1,0:T(8,128)(2,1)}, u32[]{:S(2)}) copy-start(bf16[48,512]{1,0:T(8,128)(2,1)} %param.48) | copy-start | bytes 147460
  1390.5 82.2 %copy-start.206 = (bf16[512,48]{0,1:T(8,128)(2,1)S(1)}, bf16[512,48]{0,1:T(8,128)(2,1)}, u32[]{:S(2)}) copy-start(bf16[512,48]{0,1:T(8,128)(2,1)} %param.46) | copy-start | bytes 147460
  1392.6 824.0 %all-reduce.27.cloned.1.call-start = ((), (), s32[]{:S(2)}) async-start(), calls=%async_computation.4 | async-start | bytes 14024704 | tf_op jit(solution)/shard_map/psum | solution.py:393
  1472.9 69.8 %copy-start.163 = (f32[512]{0:T(512)S(1)}, f32[512]{0:T(512)}, u32[]{:S(2)}) copy-start(f32[512]{0:T(512)} %mul.1066) | copy-start | bytes 6148
  1911.2 23.3 %collective-permute-start.10 = (bf16[64,11,1,512]{3,0,2,1:T(8,128)(2,1)S(1)}, bf16[64,11,1,512]{3,0,2,1:T(8,128)(2,1)S(1)}, u32[]{:S(2)}, u32[]{:S(2)}) collective-permute-start(bf16[64,11,1,512]{3,0,2,1:T(8,128)(2,1)S(1)} %copy.627), channel_id=1, source_target_pairs={{8,0},{16,8},{24,16},{9,1},{17,9},{25,17},{10,2},{18,10},{26,18},{... | collective-permute-start | bytes 2162696 | tf_op jit(solution)/shard_map/ppermute | solution.py:32
  1940.0 18.0 collective-permute-start.11
  1960.6 78.5 %copy-start.162 = (f32[512]{0:T(512)S(1)}, f32[512]{0:T(512)}, u32[]{:S(2)}) copy-start(f32[512]{0:T(512)} %mul.1063) | copy-start | bytes 6148
  (195 other events, 1870.1 us)
Sparse Core Ops, SparseCore 0:
  300.3 76.9 all-reduce.18
  699.6 78.0 all-reduce.20
  926.6 78.1 all-reduce.22
  1392.7 78.1 all-reduce.24
  2054.2 162.3 all-reduce.26
where the time goes:
time: 2250 us; the launch traced here: 2240 us
  blocking collectives  768 us (34%)
  waiting for transfers between devices  454 us (20%)
  local copies, waits for them, and re-layouts  428 us (19%)
  other arithmetic  302 us (13%)
  matrix products  246 us (11%)
    psum x6, blocking collectives, moments(): totals, squares = lax.psum((totals, squares), ('ha', 'wa', 'img'))  389 us
    psum x6, blocking collectives, moment_grads(): return lax.psum((shift_sums, gain_sums), ('ha', 'wa', 'img'))  379 us
    psum x4, waiting for transfers between devices, image_sums(): lax.psum(jnp.sum(field, axis=(1, 2)).astype(jnp.bfloat16), ('ha', 'wa'))  260 us
    scatter-add x9, other arithmetic, spread(): canvas = canvas.at[:, tap_row:tap_row + 2 * rows_out - 1:2, tap_col:tap_c...  163 us
    psum x1, waiting for transfers between devices, body(): lax.psum((entry_grad, group_grad, squeeze_grad, squeeze_bias_grad, excite...  141 us
    dot_general x27, matrix products, taps(): jnp.einsum(formula, window, kernel[tap_row, tap_col], preferred_element_t...  117 us
    transpose x9, local copies, waits for them, and re-layouts, spread(): jnp.einsum(BACKWARD, gradient, kernel[tap_row, tap_col], preferred_elemen...  77.9 us
    slice x3, local copies, waits for them, and re-layouts, taps(): field[:, tap_row:tap_row + stride * (rows_out - 1) + 1:stride, tap_col:ta...  72.1 us
  transfers between devices with their start and end apart: 17, of which 16 were waited for; matrix products, arithmetic and copies ran while one was open for 6% of the time, Pallas kernels for 0%

commit v1 on v0

v1 whole, which is shorter than its diff:
```python
import functools
import types

import jax
import jax.numpy as jnp
from jax import lax
from jax.experimental import pallas as pl
from jax.experimental.pallas import tpu as pltpu
from jax.sharding import PartitionSpec as P

EPS = 1e-05
F32 = jnp.float32
BF16 = jnp.bfloat16
MESH = pl.DeviceIdType.MESH
FAR = 1 << 20
LANES = 128

(
    ENTRY_G, ENTRY_S, GROUP_G, GROUP_S, OUTPUT_G, OUTPUT_S, SHORT_G, SHORT_S, SECOND_G, SECOND_S,
    SPATIAL_G, SPATIAL_S, FINAL_G, FINAL_S, EXCITE_B, EXPAND_B, SQUEEZE_B, REDUCE_B,
) = range(18)

A_, S_, B_, C_, D_, E_, F_ = range(7)
(SUM_A, SUM_B, SUM_C, SUM_D, SUM_E, SUM_F, BACK_F, BACK_E, BACK_D, BACK_C, BACK_B, BACK_A) = range(12)
VECTORS = (4, 2, 2, 2, 2, 2, 2, 2, 2, 3, 2, 2)

PARITY_TAPS = (4, 3, 5, 1, 7, 0, 2, 6, 8)
PARITY_SPANS = {(0, 0): (0, 1), (0, 1): (1, 3), (1, 0): (3, 5), (1, 1): (5, 9)}


def mm(a, b):
    return lax.dot_general(a, b, (((1,), (0,)), ((), ())), preferred_element_type=F32)


def mt(a, b):
    return lax.dot_general(a, b, (((1,), (1,)), ((), ())), preferred_element_type=F32)


def tm(a, b):
    return lax.dot_general(a, b, (((0,), (0,)), ((), ())), preferred_element_type=F32)


def exact_tm(a, b):
    return lax.dot_general(
        a, b, (((0,), (0,)), ((), ())), precision=lax.Precision.HIGHEST, preferred_element_type=F32
    )


def split_rows(a):
    high = a.astype(BF16)
    return jnp.concatenate([high, (a - high.astype(F32)).astype(BF16)], axis=0)


def fine(product, a, b):
    both = product(split_rows(a), b)
    return both[: a.shape[0]] + both[a.shape[0] :]


def fold(v):
    return jnp.sum(v.reshape(v.shape[0] // 8, 8, v.shape[1]), axis=0)


def sigmoid(v):
    return 0.5 * jnp.tanh(0.5 * v) + 0.5


def silu_half(y):
    return y * jnp.tanh(y) + y


def silu_and_slope(y):
    t = jnp.tanh(y)
    u = y * t
    return y + u, (1.0 + t) * (1.0 + (y - u))


def in_parts(v, count):
    parts = []
    for _ in range(count):
        parts.append(v.astype(BF16))
        v = v - parts[-1].astype(F32)
    return parts


def exact(product, a, b):
    (a_high, a_low), (b_high, b_low) = in_parts(a, 2), in_parts(b, 2)
    return product(a_high, b_high) + (product(a_low, b_high) + product(a_high, b_low))


def spread_lanes(m, width):
    whole, rest = divmod(width, LANES)
    parts = [m] * whole + ([m[:, :rest]] if rest else [])
    return parts[0] if len(parts) == 1 else jnp.concatenate(parts, axis=1)


def grad_rows(channels, inputs, hidden_one, hidden_two, width):
    groups = (
        dict(final=channels, reduce=hidden_two, expand=hidden_two, spatial=9 * width),
        dict(
            second=channels, output=channels, shortcut=inputs, squeeze=hidden_one, excite=hidden_one, biases=16
        ),
        dict(group=9 * width),
        dict(entry=inputs),
    )
    at, rows, jobs = 0, {}, []
    for group in groups:
        first = at
        for name, size in group.items():
            rows[name] = (at, size)
            at += size
        at = first + -(-(at - first) // LANES) * LANES
        jobs.append((first, at - first))
    return rows, jobs, at


def kernel(d, *refs):
    s = types.SimpleNamespace(**dict(zip(d.names, refs, strict=True)))
    n, c, ci, r_out, nch = d.images, d.channels, d.inputs, d.rows, d.channels // LANES
    ca = d.augmented
    half = min(256, c)
    halves = c // half
    width = d.width
    h_in = 2 * r_out
    block = r_out * n
    points = r_out * block
    group = n // d.ha
    plane = d.ha * d.wa
    chips = d.img // 2
    ha, wa, img = lax.axis_index("ha"), lax.axis_index("wa"), lax.axis_index("img")
    core, chip = img % 2, img // 2
    here = ha * d.wa + wa
    row0, col0 = ha * h_in, wa * h_in
    along_z = [ha] + [(ha + i) % d.ha for i in range(1, d.ha)]
    along_y = [wa] + [(wa + i) % d.wa for i in range(1, d.wa)]
    along_img = [img] + [(img + i) % d.img for i in range(1, d.img)]
    along_x = [2 * ((chip + i) % chips) + core for i in range(1, chips)]
    plane_peers = [(z, y) for z in along_z for y in along_y][1:]
    partner = (ha, wa, img + 1 - 2 * core)

    at = types.SimpleNamespace(**{name: first for name, (first, _) in d.grad_rows.items()})


    def beside(dr, dc):
        return (along_z[dr % d.ha], along_y[dc % d.wa], img)

    def place(g, total):
        return jnp.where(jnp.logical_or(g < 0, g >= total), FAR, g)

    def mask_at(gr, gc, lanes, value=1.0):
        far = jnp.maximum(place(gr, d.ha * h_in), place(gc, d.wa * h_in))
        return spread_lanes(jnp.where(s.lim[...] > far, value, 0.0).astype(F32), lanes)

    def masks_out(r, value=1.0):
        return [mask_at(row0 + 2 * r, col0 + 2 * j, half, value) for j in range(r_out)]

    def rows(r):
        return pl.ds(pl.multiple_of(r * block, block), block)

    def spot(r, j):
        return pl.ds(pl.multiple_of(r * block + j * n, n), n)

    def lanes(k):
        return slice(k * half, (k + 1) * half)

    def quarter(q):
        return slice(q * LANES, (q + 1) * LANES)

    def part(v, j):
        return v[j * n : (j + 1) * n]

    def vec(i):
        return s.vec[i : i + 1, :]

    pieces = [(j, k) for k in range(halves) for j in range(r_out)]

    def over(folds, images, body, steps=r_out):
        def step(r, carry):
            held = list(carry)

            def add(i, k, v):
                held[i * halves + k] = held[i * halves + k] + fold(v)

            def add_image(i, k, v):
                held[(folds + i) * halves + k] = held[(folds + i) * halves + k] + v

            body(r, add, add_image)
            return tuple(held)

        start = (jnp.zeros((8, half), F32),) * (folds * halves) + (jnp.zeros((n, half), F32),) * (images * halves)
        out = lax.fori_loop(0, steps, step, start)
        return [jnp.concatenate(out[i * halves : (i + 1) * halves], axis=1) for i in range(folds + images)]

    def over_rows(count, body):
        return over(count, 0, lambda r, add, _: body(r, add))

    def each_row(body, steps=r_out, first=0):
        def step(r, carry):
            body(r)
            return carry

        lax.fori_loop(first, steps, step, 0)


    def vector_rows(k):
        return -(-2 * nch // 8) * 8 * (2 if k in wide else 1)

    wide = [k for k, count in enumerate(VECTORS) if count > 2]

    def places_of(k):
        if k in wide:
            return s.slots_wide.at[wide.index(k)], s.across_wide.at[wide.index(k)]
        return s.slots.at[k], s.across.at[k]

    def sum_start(k, parts):
        slots, _ = places_of(k)
        lines = vector_rows(k)
        if lines > len(parts) * nch:
            slots[here] = jnp.zeros((lines, LANES), F32)
        for j, value in enumerate(parts):
            total = jnp.sum(value, axis=0, keepdims=True)
            for i in range(nch):
                line = j * nch + i
                slots[here, line : line + 1, :] = total[:, i * LANES : (i + 1) * LANES]
        mine = slots.at[here]
        for z, y in plane_peers:
            pltpu.make_async_remote_copy(
                src_ref=mine, dst_ref=mine, send_sem=s.sum_sems.at[k, 0], recv_sem=s.sum_sems.at[k, 1],
                device_id=(z, y, img), device_id_type=MESH,
            ).start()

    def sum_wait(k, sem):
        got = places_of(k)[0].at[pl.ds(0, plane - 1)]
        pltpu.make_async_copy(got, got, s.sum_sems.at[k, sem]).wait()

    def sum_wait_across(k, sem):
        got = places_of(k)[1].at[pl.ds(0, d.img - 1)]
        pltpu.make_async_copy(got, got, s.sum_sems.at[k, sem]).wait()

    def sum_finish(k):
        slots, across = places_of(k)
        lines = vector_rows(k)
        sum_wait(k, 1)
        total = slots[0]
        for i in range(1, plane):
            total = total + slots[i]
        across[img] = total
        mine = across.at[img]
        for x in along_img[1:]:
            pltpu.make_async_remote_copy(
                src_ref=mine, dst_ref=mine, send_sem=s.sum_sems.at[k, 2], recv_sem=s.sum_sems.at[k, 3],
                device_id=(ha, wa, x), device_id_type=MESH,
            ).start()
        sum_wait_across(k, 3)
        total = across[0]
        for i in range(1, d.img):
            total = total + across[i]
        s.reduced[0:lines, :] = total
        return [
            jnp.concatenate([s.reduced[j * nch + i : j * nch + i + 1, :] for i in range(nch)], axis=1)
            for j in range(VECTORS[k])
        ]

    def keep(m, i, k=None):
        return s.keep[8 * m + i : 8 * m + i + 1, slice(None) if k is None else lanes(k)]

    def set_norm(m, total, square, inverse, gain, shift):
        center = total * inverse
        factor = lax.rsqrt(square * inverse - center * center + EPS)
        scale = factor * vec(gain)
        offset = vec(shift) - center * scale
        for i, value in enumerate((center, factor, 0.5 * scale, 0.5 * offset, scale)):
            s.keep[8 * m + i : 8 * m + i + 1, :] = value

    def set_back(m, shift_sum, weighted, inverse, out, raised=0.0):
        center, factor, scale = keep(m, 0), keep(m, 1), keep(m, 4)
        gain_sum = (weighted - (center + raised) * shift_sum) * factor
        slope = -(scale * factor * gain_sum * inverse)
        offset = -(scale * shift_sum * inverse) - slope * center
        for i, value in enumerate((scale, slope, offset)):
            s.keep[8 * m + 5 + i : 8 * m + 6 + i, :] = value
        s.vectors[out : out + 1, :] = gain_sum
        s.vectors[out + 1 : out + 2, :] = shift_sum

    def back(m, upstream, field, mask, k):
        return (upstream * keep(m, 5, k) + (field * keep(m, 6, k) + keep(m, 7, k)) * mask).astype(BF16)


    def tiles_start(e, terms):
        s.tile_slots[e, here, :, 0 : terms.shape[1]] = terms.astype(BF16)
        mine = s.tile_slots.at[e, here]
        for z, y in plane_peers:
            pltpu.make_async_remote_copy(
                src_ref=mine, dst_ref=mine, send_sem=s.tile_sems.at[e, 0], recv_sem=s.tile_sems.at[e, 1],
                device_id=(z, y, img), device_id_type=MESH,
            ).start()

    def tiles_wait(e, sem):
        got = s.tile_slots.at[e, pl.ds(0, plane - 1)]
        pltpu.make_async_copy(got, got, s.tile_sems.at[e, sem]).wait()

    def tiles_finish(e, units):
        tiles_wait(e, 1)
        total = s.tile_slots[e, 0].astype(F32)
        for i in range(1, plane):
            total = total + s.tile_slots[e, i].astype(F32)
        return total[:, 0:units]

    def gates_load(parts):
        for i, value in enumerate(parts):
            s.gate_src[:, i] = value.astype(BF16).reshape(d.ha, group, c)

    def gates_start(which):
        s.gate_slots[here] = s.gate_src[ha]
        for z, y in plane_peers:
            pltpu.make_async_remote_copy(
                src_ref=s.gate_src.at[z], dst_ref=s.gate_slots.at[here], send_sem=s.gate_sems.at[which, 0],
                recv_sem=s.gate_sems.at[which, 1], device_id=(z, y, img), device_id_type=MESH,
            ).start()

    def gates_finish(which):
        got = s.gate_slots.at[pl.ds(0, plane - 1)]
        pltpu.make_async_copy(got, got, s.gate_sems.at[which, 1]).wait()
        for i in range(2):
            total = s.gate_slots[0, i].astype(F32)
            for j in range(1, plane):
                total = total + s.gate_slots[j, i].astype(F32)
            s.gates[which, ha, i] = total
        pltpu.make_async_copy(got, got, s.gate_sems.at[which, 0]).wait()
        mine = s.gates.at[which, ha]
        for z in along_z[1:]:
            pltpu.make_async_remote_copy(
                src_ref=mine, dst_ref=mine, send_sem=s.gate_sems.at[which, 2], recv_sem=s.gate_sems.at[which, 3],
                device_id=(z, wa, img), device_id_type=MESH,
            ).start()

    def gates_wait(which, sem):
        got = s.gates.at[which, pl.ds(0, d.ha - 1)]
        pltpu.make_async_copy(got, got, s.gate_sems.at[which, sem]).wait()

    def img_wait(which, sem):
        got = s.group_x.at[which, pl.ds(0, d.img - 1)]
        pltpu.make_async_copy(got, got, s.group_sems.at[which, sem]).wait()

    def img_start(which, rows_):
        for j, row in enumerate(rows_):
            for i in range(nch):
                line = j * nch + i
                s.group_x[which, img, line : line + 1, :] = row[:, i * LANES : (i + 1) * LANES]
        mine = s.group_x.at[which, img]
        for x in along_img[1:]:
            pltpu.make_async_remote_copy(
                src_ref=mine, dst_ref=mine, send_sem=s.group_sems.at[which, 0], recv_sem=s.group_sems.at[which, 1],
                device_id=(ha, wa, x), device_id_type=MESH,
            ).start()

    def img_finish(which):
        img_wait(which, 1)
        total = s.group_x[which, 0]
        for i in range(1, d.img):
            total = total + s.group_x[which, i]
        s.reduced[0 : 2 * nch, :] = total[0 : 2 * nch]
        return [
            jnp.concatenate([s.reduced[j * nch + i : j * nch + i + 1, :] for i in range(nch)], axis=1)
            for j in range(2)
        ]

    def every(j, k):
        return s.shared[j, :, :, lanes(k)].reshape(n, half)

    def inverse_pixels():
        return spread_lanes(s.invpix[...].reshape(n, LANES), c)

    def excite_forward(j, excitation, sums):
        e = excitation
        pooled = sums * inverse_pixels()
        tiles_start(j, fine(mt if e.turned else mm, pooled, e.down[...]))
        e.pooled[...] = pooled
        before = tiles_finish(j, e.units) + vec(e.down_bias)[:, : e.units]
        e.before[...] = before
        scaling = sigmoid(fine(mm, before * sigmoid(before), e.up[...]) + vec(e.up_bias))
        s.shared[j] = scaling.reshape(d.ha, group, c)

    def excite_backward_start(j, forward, excitation, sums):
        scaling = s.shared[forward].reshape(n, c)
        dlogit = sums * scaling * (1.0 - scaling)
        tiles_start(j, fine(mt, dlogit, excitation.up[...]))
        s.dlogit[...] = dlogit

    def excite_backward(j, excitation, which):
        e = excitation
        before = e.before[...]
        logistic = sigmoid(before)
        dbefore = tiles_finish(j, e.units) * (logistic * (1.0 + before * (1.0 - logistic)))
        dpooled = fine(mm if e.turned else mt, dbefore, e.down[...]) * inverse_pixels()
        img_start(
            which,
            [jnp.sum(dpooled * s.gates[which, :, i].reshape(n, c), axis=0, keepdims=True) for i in range(2)],
        )
        s.shared[j] = dpooled.reshape(d.ha, group, c)
        dlogit = s.dlogit[...]
        s.stage[e.up_at : e.up_at + e.units, :] = exact_tm(before * logistic, dlogit).astype(BF16)
        if e.turned:
            s.stage[e.down_at : e.down_at + e.units, :] = exact_tm(dbefore, e.pooled[...]).astype(BF16)
        else:
            down = exact_tm(e.pooled[...], dbefore)
            for i in range(nch):
                s.stage[e.down_at : e.down_at + LANES, quarter(i)] = down[quarter(i)].astype(BF16)
        owner = jnp.where(here == 0, 1.0, 0.0).astype(F32)
        s.biases[e.bias_at : e.bias_at + 1, :] = jnp.sum(dlogit, axis=0, keepdims=True)
        s.biases[e.bias_at + 1 : e.bias_at + 2, 0 : e.units] = jnp.sum(dbefore, axis=0, keepdims=True) * owner

    one = types.SimpleNamespace(
        turned=True, down=s.squeeze, up=s.excite, units=d.hidden_one, down_bias=SQUEEZE_B, up_bias=EXCITE_B,
        pooled=s.pooled_one, before=s.before_one, down_at=at.squeeze, up_at=at.excite, bias_at=0,
    )
    two = types.SimpleNamespace(
        turned=False, down=s.reduce, up=s.expand, units=d.hidden_two, down_bias=REDUCE_B, up_bias=EXPAND_B,
        pooled=s.pooled_two, before=s.before_two, down_at=at.reduce, up_at=at.expand, bias_at=2,
    )


    class Reduction:
        def __init__(self, index):
            self.index = index
            self.first, self.size = d.jobs[index]
            self.direct = index == 3
            self.hr = self.size if self.direct else self.size // 2
            self.pr = self.hr // d.ha
            self.slot = pl.ds(self.first // (2 * d.ha), self.pr)
            self.mine = self.first if self.direct else self.first + core * self.hr
            self.other = self.first + (1 - core) * self.hr
            self.apart = index >= 2
            self.home = s.excited_two if self.apart else s.stage
            self.shift = d.jobs[2][0] if self.apart else 0

        def sem(self, i):
            return s.grad_sems.at[self.index, i]

        def half_at(self, ref, first):
            return ref.at[pl.ds(pl.multiple_of(first, 16), self.hr)]

        def piece(self, ref, z, y, shift=0):
            first = pl.multiple_of(self.mine - shift + z * self.pr, 16)
            return ref.at[pl.ds(first, self.pr), pl.ds(pl.multiple_of(y * LANES, LANES), LANES)]

        def wait(self, ref, sem):
            pltpu.make_async_copy(ref, ref, self.sem(sem)).wait()

        def swapped(self):
            return s.swaps.at[pl.ds(self.first // 2, self.hr)]

        def many(self):
            return s.scattered.at[pl.ds(0, plane - 1), self.slot]

        def swap(self):
            pltpu.make_async_remote_copy(
                src_ref=self.half_at(s.stage, self.other), dst_ref=self.swapped(), send_sem=self.sem(0),
                recv_sem=self.sem(1), device_id=partner, device_id_type=MESH,
            ).start()

        def scatter(self):
            lines = min(32, self.pr)

            def add(i):
                mine = pl.ds(pl.multiple_of(self.mine + i * lines, 16), lines)
                theirs = pl.ds(pl.multiple_of(self.first // 2 + i * lines, 16), lines)
                s.stage[mine, :] = (s.stage[mine, :].astype(F32) + s.swaps[theirs, :].astype(F32)).astype(BF16)

            if not self.direct:
                self.wait(self.swapped(), 1)
                each_row(add, self.hr // lines)
            for z, y in plane_peers:
                pltpu.make_async_remote_copy(
                    src_ref=self.piece(s.stage, z, y), dst_ref=s.scattered.at[here, self.slot],
                    send_sem=self.sem(2), recv_sem=self.sem(3), device_id=(z, y, img), device_id_type=MESH,
                ).start()
            s.scattered[here, self.slot] = self.piece(s.stage, ha, wa)[...]

        def level(self):
            if self.direct:
                return s.crossed_all, img, d.img, pl.ds(0, self.pr), along_img[1:]
            return s.crossed, chip, chips, self.slot, along_x

        def exchange(self):
            self.wait(self.many(), 3)
            places, own, _, slot, peers = self.level()

            def add(i):
                lines = pl.ds(pl.multiple_of(self.slot.start + i * 16, 16), 16)
                total = s.scattered[0, lines].astype(F32)
                for j in range(1, plane):
                    total = total + s.scattered[j, lines].astype(F32)
                places[own, pl.ds(pl.multiple_of(slot.start + i * 16, 16), 16)] = total.astype(BF16)

            each_row(add, self.pr // 16)
            mine = places.at[own, slot]
            for x in peers:
                pltpu.make_async_remote_copy(
                    src_ref=mine, dst_ref=mine, send_sem=self.sem(4), recv_sem=self.sem(5),
                    device_id=(ha, wa, x), device_id_type=MESH,
                ).start()

        def wait_crossing(self, sem):
            places, _, count, slot, _ = self.level()
            if count > 1:
                self.wait(places.at[pl.ds(0, count - 1), slot], sem)

        def gather(self):
            self.wait_crossing(5)
            places, _, count, slot, _ = self.level()

            def add(i):
                lines = pl.ds(pl.multiple_of(slot.start + i * 16, 16), 16)
                total = places[0, lines].astype(F32)
                for j in range(1, count):
                    total = total + places[j, lines].astype(F32)
                s.summed[pl.ds(pl.multiple_of(self.slot.start + i * 16, 16), 16)] = total.astype(BF16)

            each_row(add, self.pr // 16)
            mine = self.piece(self.home, ha, wa, self.shift)
            mine[...] = s.summed[self.slot]
            for z, y in plane_peers:
                pltpu.make_async_remote_copy(
                    src_ref=s.summed.at[self.slot], dst_ref=mine, send_sem=self.sem(6), recv_sem=self.sem(7),
                    device_id=(z, y, img), device_id_type=MESH,
                ).start()

        def hand(self):
            self.wait(self.many(), 7)
            if self.direct:
                return
            mine = self.half_at(self.home, self.mine - self.shift)
            pltpu.make_async_remote_copy(
                src_ref=mine, dst_ref=mine, send_sem=self.sem(8), recv_sem=self.sem(9),
                device_id=partner, device_id_type=MESH,
            ).start()

        def finish(self):
            if not self.direct:
                self.wait(self.half_at(self.home, self.other - self.shift), 9)
                self.wait(self.half_at(self.home, self.mine - self.shift), 8)
            self.wait(self.many(), 6)
            self.wait_crossing(4)
            if self.apart:
                self.settle()
                lines = min(32, self.size)

                def bring(i):
                    there = pl.ds(pl.multiple_of(self.first + i * lines, 16), lines)
                    here_ = pl.ds(pl.multiple_of(self.first - self.shift + i * lines, 16), lines)
                    s.stage[there, :] = s.excited_two[here_, :]

                each_row(bring, self.size // lines)

        def settle(self):
            self.wait(self.many(), 2)
            if not self.direct:
                self.wait(self.half_at(s.stage, self.other), 0)

    jobs = [Reduction(i) for i in range(len(d.jobs))]


    around = [(dr, dc) for dr in (-1, 0, 1) for dc in (-1, 0, 1) if (dr, dc) != (0, 0)]

    def edge(step):
        if step == 0:
            return pl.ds(1, r_out), pl.ds(1, r_out)
        return (pl.ds(r_out, 1), pl.ds(0, 1)) if step > 0 else (pl.ds(1, 1), pl.ds(r_out + 1, 1))

    def ring_copies(frame, h):
        copies = []
        for i, (dr, dc) in enumerate(around):
            (from_r, to_r), (from_c, to_c) = edge(dr), edge(dc)
            copies.append(
                pltpu.make_async_remote_copy(
                    src_ref=frame.at[from_r, from_c], dst_ref=frame.at[to_r, to_c],
                    send_sem=s.ring_send.at[h, i], recv_sem=s.ring_recv.at[h, i],
                    device_id=beside(dr, dc), device_id_type=MESH,
                )
            )
        return copies

    def three_copies(parts, send, recv):
        return [
            pltpu.make_async_remote_copy(
                src_ref=src, dst_ref=dst, send_sem=send.at[i], recv_sem=recv.at[i],
                device_id=beside(*to), device_id_type=MESH,
            )
            for i, (src, dst, to) in enumerate(parts)
        ]

    def rim_copies():
        last = h_in - 1
        parts = (
            (s.images.at[last], s.rim.at[0], (1, 0)),
            (s.images.at[pl.ds(0, h_in), last], s.rim.at[1], (0, 1)),
            (s.images.at[last, pl.ds(last, 1)], s.rim_corner, (1, 1)),
        )
        return three_copies(parts, s.rim_send, s.rim_recv)

    def corner_copies(frame):
        first, all_, last = pl.ds(0, 1), pl.ds(0, r_out), pl.ds(r_out, 1)
        parts = (
            (frame.at[first, all_], frame.at[last, all_], (-1, 0)),
            (frame.at[all_, first], frame.at[all_, last], (0, -1)),
            (frame.at[first, first], frame.at[last, last], (-1, -1)),
        )
        return three_copies(parts, s.corner_send, s.corner_recv)


    def same_group():
        down = lax.broadcasted_iota(jnp.int32, (half, half), 0) // width
        across = lax.broadcasted_iota(jnp.int32, (half, half), 1) // width
        return jnp.where(down == across, 1.0, 0.0).astype(F32)

    def block_diagonal(source, t, k, same):
        return jnp.concatenate([source[t, :, lanes(k)]] * (half // width), axis=0) * same

    def build_kernel(source):
        same = same_group().astype(BF16)

        def tap(t):
            for k in range(halves):
                s.taps[k, pl.ds(pl.multiple_of(t * half, half), half), :] = block_diagonal(source, t, k, same)

        each_row(tap, 9)

    def build_turned(source, order):
        same = same_group().astype(BF16)
        for i, t in enumerate(order):
            for k in range(halves):
                s.taps[k, i * half : (i + 1) * half, :] = block_diagonal(source, t, k, same).T

    def kernel_grad(dz, window, first):
        down = lax.broadcasted_iota(jnp.int32, (LANES, LANES), 0) // width
        across = lax.broadcasted_iota(jnp.int32, (LANES, LANES), 1) // width
        same = jnp.where(down == across, 1.0, 0.0).astype(F32)
        for q in range(nch):
            s.turned[q] = dz(q).T

        def pair(t):
            taps = [2 * t, jnp.minimum(2 * t + 1, 8)]
            for q in range(nch):
                windows = [window(tap // 3, tap % 3, q) for tap in taps]
                got = mm(s.turned[q], jnp.concatenate(windows, axis=1)).T
                for i, tap in enumerate(taps):
                    block_ = got[i * LANES : (i + 1) * LANES] * same
                    total = block_[0:width]
                    for g in range(1, LANES // width):
                        total = total + block_[g * width : (g + 1) * width]
                    there = pl.ds(pl.multiple_of(first + tap * width, 16), width)
                    s.stage[there, quarter(q)] = total.astype(BF16)

        each_row(pair, 5)

    def product_grad(left, columns, first):
        def some(j):
            span = pl.ds(pl.multiple_of(j * LANES, LANES), LANES)
            got = tm(left(span), s.cot[...].reshape(points, c))
            s.stage[pl.ds(pl.multiple_of(first + j * LANES, 16), LANES), :] = got.astype(BF16)

        each_row(some, columns // LANES)

    def strided(i, ph, pw):
        return jnp.concatenate([s.x[2 * i + ph, 2 * j + pw] for j in range(r_out)], axis=0)

    def bypass(sources, k):
        return mm(sources, s.short_rows[:, lanes(k)])

    def augment(raw, gr, gc):
        mask = mask_at(gr, gc, LANES)
        lane = lax.broadcasted_iota(jnp.int32, (n, ca - ci), 1)
        more = jnp.where(lane < 3, mask[:, : ca - ci], 0.0)
        return jnp.concatenate([raw.astype(F32) * spread_lanes(mask, ci), more], axis=1).astype(BF16)

    def below(value_rows):
        row = lax.broadcasted_iota(jnp.int32, (ca - ci, c), 0)
        total = jnp.zeros((ca - ci, c), F32)
        for i, value in enumerate(value_rows):
            total = jnp.where(row == i, value.astype(F32), total)
        return total

    def gram_moments(gram, kernel_rows):
        parts = in_parts(gram[0:ci, 0:ci], 3)
        product = sum(mm(p, kernel_rows[...]) for p in parts)
        square = jnp.sum(product * kernel_rows[...].astype(F32), axis=0, keepdims=True)
        total = sum(mm(p, kernel_rows[...]) for p in in_parts(gram[ci : ci + 16, 0:ci], 3))[0:1]
        return total, square

    def residual_row(r):
        return s.residual[r + 1, pl.ds(1, r_out)].reshape(block, c)

    def augment(raw, gr, gc):
        mask = mask_at(gr, gc, LANES)
        lane = lax.broadcasted_iota(jnp.int32, (n, ca - ci), 1)
        more = jnp.where(lane < 3, mask[:, : ca - ci], 0.0)
        return jnp.concatenate([raw.astype(F32) * spread_lanes(mask, ci), more], axis=1).astype(BF16)

    def below(value_rows):
        row = lax.broadcasted_iota(jnp.int32, (ca - ci, c), 0)
        total = jnp.zeros((ca - ci, c), F32)
        for i, value in enumerate(value_rows):
            total = jnp.where(row == i, value.astype(F32), total)
        return total

    def gram_moments(gram, kernel_rows):
        parts = in_parts(gram[0:ci, 0:ci], 3)
        product = sum(mm(p, kernel_rows[...]) for p in parts)
        square = jnp.sum(product * kernel_rows[...].astype(F32), axis=0, keepdims=True)
        total = sum(mm(p, kernel_rows[...]) for p in in_parts(gram[ci : ci + 16, 0:ci], 3))[0:1]
        return total, square

    def residual_row(r):
        return s.residual[r + 1, pl.ds(1, r_out)].reshape(block, c)

    def second(r, k):
        return mm(residual_row(r), s.second_kernel[:, lanes(k)])


    depth = s.raw.shape[0]

    def load(h):
        return pltpu.make_async_copy(s.images.at[h], s.raw.at[h % depth], s.load_sems.at[h % depth])

    for h in range(depth):
        load(h).start()
    cot_load = pltpu.make_async_copy(s.cotangent, s.cot, s.cot_sem.at[0])
    cot_load.start()
    vec_loads = [
        pltpu.make_async_copy(getattr(s, name), s.vec.at[i, pl.ds(0, size)], s.vec_sems.at[i])
        for i, (name, size) in enumerate(d.vectors)
    ]
    for copy in vec_loads:
        copy.start()

    barrier = pltpu.get_barrier_semaphore()
    for z, y in plane_peers:
        pl.semaphore_signal(barrier, inc=1, device_id=(z, y, img), device_id_type=MESH)
    for x in along_img[1:]:
        pl.semaphore_signal(barrier, inc=1, device_id=(ha, wa, x), device_id_type=MESH)

    classes = s.classes[...]
    slot = lax.broadcasted_iota(jnp.int32, classes.shape, 1)
    side = 10 + 4 * classes
    index = lax.broadcasted_iota(jnp.int32, classes.shape, 0)
    counts = jnp.zeros(classes.shape, jnp.int32)
    for i in range(d.img):
        counts = jnp.where(index == i, s.image_counts[i], counts)
    cells = jnp.sum(jnp.where(slot < counts, (side * side).astype(F32), 0.0), axis=1, keepdims=True)
    inv_out = 1.0 / jnp.sum(cells, axis=0, keepdims=True)
    inv_in = 0.25 * inv_out
    own_side = (10 + 4 * s.classes[pl.ds(img, 1), :]).astype(F32)
    spread = jnp.broadcast_to(own_side, (n, n))
    diagonal = lax.broadcasted_iota(jnp.int32, (n, n), 0) == lax.broadcasted_iota(jnp.int32, (n, n), 1)
    sides = jnp.sum(jnp.where(diagonal, spread, 0.0), axis=1, keepdims=True)
    sides = jnp.broadcast_to(sides, (n, LANES))
    alive = lax.broadcasted_iota(jnp.int32, (n, LANES), 0) < s.image_counts[img]
    s.lim[...] = jnp.where(alive, 2.0 * sides, 0.0).astype(jnp.int32)
    s.invpix[...] = (1.0 / (sides * sides)).reshape(d.ha, group, LANES)
    s.biases[...] = jnp.zeros((16, c), F32)

    pl.semaphore_wait(barrier, plane - 1 + d.img - 1)
    rims = rim_copies()
    for copy in rims:
        copy.start()

    s.gram[...] = jnp.zeros((ca, ca), F32)
    s.gathered[:, 0:ca] = jnp.zeros((ca, ca), F32)

    def load_rows(i):
        for h in (2 * i, 2 * i + 1):
            load(h).wait()
            for w in range(h_in):
                s.x[h, w] = augment(s.raw[h % depth, w], row0 + h, col0 + w)

            @pl.when(h + depth < h_in)
            def _(h=h):
                load(h + depth).start()

            x = s.x[h].reshape(h_in * n, ca)
            s.gram[...] += tm(x, x)
        x = strided(i, 0, 0)
        s.gathered[:, 0:ca] += tm(x, x)

    each_row(load_rows)
    sums_a = gram_moments(s.gram, s.entry_kernel)
    sum_start(SUM_A, sums_a + gram_moments(s.gathered, s.shortcut_kernel))
    build_kernel(s.group_kernel)
    s.entry_rows[0:ci, :] = s.entry_kernel[...]
    s.short_rows[0:ci, :] = s.shortcut_kernel[...]
    s.short_rows[ci:ca, :] = jnp.zeros((ca - ci, c), BF16)
    for copy in vec_loads:
        copy.wait()
    total_a, square_a, total_s, square_s = sum_finish(SUM_A)
    set_norm(A_, total_a, square_a, inv_in, ENTRY_G, ENTRY_S)
    set_norm(S_, total_s, square_s, inv_out, SHORT_G, SHORT_S)
    raised = vec(ENTRY_S) / keep(A_, 4) - keep(A_, 0)
    s.entry_rows[ci:ca, :] = below(in_parts(raised, 3)).astype(BF16)

    def activate(x, count, store):
        for k in range(halves):
            entry = mm(x, s.entry_rows[:, lanes(k)])
            for j in range(count):
                store(j, k, silu_half(part(entry, j) * keep(A_, 2, k)).astype(BF16))

    def active_row(h):
        for q in range(2):
            def store(j, k, value, q=q):
                s.active[h + 1, 1 + r_out * q + j, :, lanes(k)] = value

            activate(s.x[h, pl.ds(r_out * q, r_out)].reshape(block, ca), r_out, store)

    each_row(active_row, h_in)
    for copy in rims:
        copy.wait_recv()

    for q in range(2):
        def store_top(j, k, value, q=q):
            s.active[0, 1 + r_out * q + j, :, lanes(k)] = value

        def store_left(j, k, value, q=q):
            s.active[1 + r_out * q + j, 0, :, lanes(k)] = value

        for j in range(r_out):
            s.rim_rows[j] = augment(s.rim[0, r_out * q + j], row0 - 1, col0 + r_out * q + j)
        activate(s.rim_rows[...].reshape(block, ca), r_out, store_top)
        for j in range(r_out):
            s.rim_rows[j] = augment(s.rim[1, r_out * q + j], row0 + r_out * q + j, col0 - 1)
        activate(s.rim_rows[...].reshape(block, ca), r_out, store_left)

    def store_corner(j, k, value):
        s.active[0, 0, :, lanes(k)] = value

    activate(augment(s.rim_corner[0], row0 - 1, col0 - 1), 1, store_corner)


    def convolve(window, store):
        def row(r, add):
            masks = masks_out(r)
            for k in range(halves):
                windows = [window(r, ky, kx, k) for ky in range(3) for kx in range(3)]
                field = mm(jnp.concatenate(windows, axis=1), s.taps[k])
                store[rows(r), lanes(k)] = field.astype(BF16)
                for j in range(r_out):
                    masked = part(field, j) * masks[j]
                    add(0, k, masked)
                    add(1, k, masked * part(field, j))

        return over_rows(2, row)

    def window_one(r, ky, kx, k):
        return jnp.concatenate([s.active[2 * r + ky, 2 * j + kx, :, lanes(k)] for j in range(r_out)], axis=0)

    sum_start(SUM_B, convolve(window_one, s.middle))
    build_kernel(s.spatial_kernel)
    set_norm(B_, *sum_finish(SUM_B), inv_out, GROUP_G, GROUP_S)

    def gated(m, store, r, j, k, mask):
        return silu_half(store[spot(r, j), lanes(k)].astype(F32) * keep(m, 2, k) + keep(m, 3, k)) * mask

    def gated_sums(m, store):
        def row(r, add, add_image):
            masks, masks_half = masks_out(r), masks_out(r, 0.5)
            for j, k in pieces:
                field = store[spot(r, j), lanes(k)].astype(F32)
                value, slope = silu_and_slope(field * keep(m, 2, k) + keep(m, 3, k))
                slope = slope * masks_half[j]
                add_image(0, k, value * masks[j])
                add_image(1, k, slope)
                add_image(2, k, slope * field)

        return over(0, 3, row)

    def excite_row(r, m, store, forward, excited):
        masks = masks_out(r)
        for j, k in pieces:
            value = gated(m, store, r, j, k, masks[j]) * every(forward, k)
            excited[spot(r, j), lanes(k)] = value.astype(BF16)

    pooled_sums, *gate_sums = gated_sums(B_, s.middle)
    excite_forward(0, one, pooled_sums)
    gates_load(gate_sums)

    def branch_row(r, add):
        excite_row(r, B_, s.middle, 0, s.excited_one)
        for k in range(halves):
            field = mm(s.excited_one[rows(r), :], s.output_kernel[:, lanes(k)])
            s.branch[rows(r), lanes(k)] = field.astype(BF16)
            add(0, k, field)
            add(1, k, field * field)

    sum_start(SUM_C, over_rows(2, branch_row))
    set_norm(C_, *sum_finish(SUM_C), inv_out, OUTPUT_G, OUTPUT_S)


    def total_one_half(field, skip, k):
        return field * keep(C_, 2, k) + skip * keep(S_, 2, k) + (keep(C_, 3, k) + keep(S_, 3, k))

    def second_row(r, add):
        masks, sources = masks_out(r), strided(r, 0, 0)
        for k in range(halves):
            skip = bypass(sources, k)
            for j in range(r_out):
                field = s.branch[spot(r, j), lanes(k)].astype(F32)
                value = silu_half(total_one_half(field, part(skip, j), k)) * masks[j]
                s.residual[r + 1, 1 + j, :, lanes(k)] = value.astype(BF16)
        for k in range(halves):
            field = mm(residual_row(r), s.second_kernel[:, lanes(k)])
            s.second[rows(r), lanes(k)] = field.astype(BF16)
            add(0, k, field)
            add(1, k, field * field)

    sums_d = over_rows(2, second_row)
    ring = ring_copies(s.residual, 0)
    for copy in ring:
        copy.start()
    sum_start(SUM_D, sums_d)
    s.square_t[...] = s.final_kernel[...].T
    set_norm(D_, *sum_finish(SUM_D), inv_out, SECOND_G, SECOND_S)
    gates_start(0)

    def put_active_two(field, fr, fc, k):
        mask = mask_at(row0 + 2 * (fr - 1), col0 + 2 * (fc - 1), half)
        value = silu_half(field * keep(D_, 2, k) + keep(D_, 3, k)) * mask
        s.frame[fr, fc, :, lanes(k)] = value.astype(BF16)

    def active_two(x, places):
        for k in range(halves):
            field = mm(x, s.second_kernel[:, lanes(k)])
            for j, (fr, fc) in enumerate(places):
                put_active_two(part(field, j), fr, fc, k)

    def active_two_row(r):
        for j, k in pieces:
            put_active_two(s.second[spot(r, j), lanes(k)].astype(F32), r + 1, 1 + j, k)

    each_row(active_two_row)
    for copy in ring:
        copy.wait_recv()
    for fr in (0, r_out + 1):
        x = s.residual[fr].reshape((r_out + 2) * n, c)
        active_two(x, [(fr, fc) for fc in range(r_out + 2)])
    for fc in (0, r_out + 1):
        x = s.residual[pl.ds(1, r_out), fc].reshape(block, c)
        active_two(x, [(fr, fc) for fr in range(1, r_out + 1)])

    def window_two(r, ky, kx, k):
        return s.frame[r + ky, pl.ds(kx, r_out), :, lanes(k)].reshape(block, half)

    sum_start(SUM_E, convolve(window_two, s.spatial))
    s.start_rows[0:c, :] = s.shortcut_kernel[...].T
    gates_finish(0)
    set_norm(E_, *sum_finish(SUM_E), inv_out, SPATIAL_G, SPATIAL_S)

    pooled_sums, *gate_sums = gated_sums(E_, s.spatial)
    excite_forward(1, two, pooled_sums)
    gates_load(gate_sums)

    def final_row(r, add):
        excite_row(r, E_, s.spatial, 1, s.excited_two)
        for k in range(halves):
            field = mm(s.excited_two[rows(r), :], s.final_kernel[:, lanes(k)])
            s.field[rows(r), lanes(k)] = field
            add(0, k, field)
            add(1, k, field * field)

    sum_start(SUM_F, over_rows(2, final_row))
    cot_load.wait()
    build_turned(s.spatial_kernel, range(9))
    set_norm(F_, *sum_finish(SUM_F), inv_out, FINAL_G, FINAL_S)
    gates_start(1)


    def top_row(r, add):
        masks, masks_half = masks_out(r), masks_out(r, 0.5)
        for j, k in pieces:
            field = s.field[spot(r, j), lanes(k)]
            kept = s.residual[r + 1, 1 + j, :, lanes(k)].astype(F32)
            value, slope = silu_and_slope(field * keep(F_, 2, k) + keep(F_, 3, k) + 0.5 * kept)
            upstream = s.cot[r, j, :, lanes(k)].astype(F32) * masks_half[j] * slope
            s.cot[r, j, :, lanes(k)] = (value * masks[j]).astype(BF16)
            s.upstream[spot(r, j), lanes(k)] = upstream
            add(0, k, upstream)
            add(1, k, upstream * field)

    sum_start(BACK_F, over_rows(2, top_row))
    gates_finish(1)
    activations_out = pltpu.make_async_copy(s.cot, s.activations, s.cot_sem.at[1])
    activations_out.start()
    set_back(F_, *sum_finish(BACK_F), inv_out, FINAL_G)
    activations_out.wait()

    def excited_back(r, add, add_image, m, store, forward):
        masks, masks_half = masks_out(r), masks_out(r, 0.5)
        dz = s.cot[r].reshape(block, c)
        for k in range(halves):
            dexcited = mm(dz, s.square_t[:, lanes(k)])
            s.field[rows(r), lanes(k)] = dexcited
            for j in range(r_out):
                field = store[spot(r, j), lanes(k)].astype(F32)
                value, slope = silu_and_slope(field * keep(m, 2, k) + keep(m, 3, k))
                add_image(0, k, part(dexcited, j) * (value * masks[j]))
                upstream = part(dexcited, j) * every(forward, k) * (slope * masks_half[j])
                add(0, k, upstream)
                add(1, k, upstream * field)

    def final_back(r, add, add_image):
        masks = masks_out(r)
        for j, k in pieces:
            upstream, field = s.upstream[spot(r, j), lanes(k)], s.field[spot(r, j), lanes(k)]
            s.cot[r, j, :, lanes(k)] = back(F_, upstream, field, masks[j], k)
        excited_back(r, add, add_image, E_, s.spatial, 1)

    *sums_e, dscaling_sums = over(2, 1, final_back)
    excite_backward_start(2, 1, two, dscaling_sums)
    sum_start(BACK_E, sums_e)
    product_grad(lambda span: s.excited_two[0:points, span], c, at.final)
    gates_wait(1, 3)
    excite_backward(2, two, 1)

    def gate_back(m, forward, backward, store, put):
        def row(r):
            masks, masks_half = masks_out(r), masks_out(r, 0.5)
            for j, k in pieces:
                field = store[spot(r, j), lanes(k)].astype(F32)
                _, slope = silu_and_slope(field * keep(m, 2, k) + keep(m, 3, k))
                dgated = s.field[spot(r, j), lanes(k)] * every(forward, k) + every(backward, k)
                put(r, j, k, back(m, dgated * masks_half[j] * slope, field, masks[j], k))

        each_row(row)

    def finish_gate(k, which):
        shift_sum, weighted = sum_finish(k)
        more_shift, more_weighted = img_finish(which)
        return shift_sum + more_shift, weighted + more_weighted

    set_back(E_, *finish_gate(BACK_E, 1), inv_out, SPATIAL_G)

    def put_spatial(r, j, k, dz):
        s.dframe[r + 1, 1 + j, :, lanes(k)] = dz

    gate_back(E_, 1, 2, s.spatial, put_spatial)
    ring_back = ring_copies(s.dframe, 1)
    for copy in ring_back:
        copy.start()
    inner = pl.ds(1, r_out)
    outer = pl.ds(0, r_out)

    def all_two(ky, kx, q):
        return s.frame[pl.ds(ky, r_out), pl.ds(kx, r_out), :, quarter(q)].reshape(points, LANES)

    kernel_grad(lambda q: s.dframe[inner, inner, :, quarter(q)].reshape(points, LANES), all_two, at.spatial)
    for copy in ring_back:
        copy.wait_recv()
    blank = jnp.zeros((r_out + 2, n, c), BF16)

    @pl.when(ha == 0)
    def _():
        s.dframe[0] = blank

    @pl.when(ha == d.ha - 1)
    def _():
        s.dframe[r_out + 1] = blank

    @pl.when(wa == 0)
    def _():
        s.dframe[:, 0] = blank

    @pl.when(wa == d.wa - 1)
    def _():
        s.dframe[:, r_out + 1] = blank

    def second_back(r, add):
        masks = masks_out(r, 0.5)
        for k in range(halves):
            windows = [
                s.dframe[r + 2 - ky, pl.ds(2 - kx, r_out), :, lanes(k)].reshape(block, half)
                for ky in range(3)
                for kx in range(3)
            ]
            total = mm(jnp.concatenate(windows, axis=1), s.taps[k])
            for j in range(r_out):
                field = s.second[spot(r, j), lanes(k)].astype(F32)
                _, slope = silu_and_slope(field * keep(D_, 2, k) + keep(D_, 3, k))
                upstream = part(total, j) * masks[j] * slope
                s.field[spot(r, j), lanes(k)] = upstream
                add(0, k, upstream)
                add(1, k, upstream * field)

    sum_start(BACK_D, over_rows(2, second_back))
    jobs[0].swap()
    build_turned(s.group_kernel, PARITY_TAPS)
    s.square_t[...] = s.second_kernel[...].T
    set_back(D_, *sum_finish(BACK_D), inv_out, SECOND_G)


    def residual_back(r, add):
        masks, masks_half, sources = masks_out(r), masks_out(r, 0.5), strided(r, 0, 0)
        for j, k in pieces:
            upstream, field = s.field[spot(r, j), lanes(k)], s.second[spot(r, j), lanes(k)].astype(F32)
            s.cot[r, j, :, lanes(k)] = back(D_, upstream, field, masks[j], k)
        dz = s.cot[r].reshape(block, c)
        for k in range(halves):
            dresidual, skips = mm(dz, s.square_t[:, lanes(k)]), bypass(sources, k)
            for j in range(r_out):
                field, skip = s.branch[spot(r, j), lanes(k)].astype(F32), part(skips, j)
                _, slope = silu_and_slope(total_one_half(field, skip, k))
                upstream = (s.upstream[spot(r, j), lanes(k)] + part(dresidual, j)) * masks_half[j] * slope
                s.field[spot(r, j), lanes(k)] = upstream
                add(0, k, upstream)
                add(1, k, upstream * field)
                add(2, k, upstream * skip)

    sum_start(BACK_C, over_rows(3, residual_back))
    product_grad(lambda span: s.residual[inner, inner, :, span].reshape(points, LANES), c, at.second)
    jobs[0].scatter()
    s.square_t[...] = s.output_kernel[...].T
    shift_c, gain_c, gain_s = sum_finish(BACK_C)
    set_back(C_, shift_c, gain_c, inv_out, OUTPUT_G)
    set_back(S_, shift_c, gain_s, inv_out, SHORT_G)

    s.gathered[...] = jnp.zeros((ca, c), F32)

    def branch_back(r, add, add_image):
        masks, sources = masks_out(r), strided(r, 0, 0)
        for k in range(halves):
            skips = bypass(sources, k)
            for j in range(r_out):
                upstream, field = s.field[spot(r, j), lanes(k)], s.branch[spot(r, j), lanes(k)].astype(F32)
                s.cot[r, j, :, lanes(k)] = back(C_, upstream, field, masks[j], k)
                s.skip[j * n : (j + 1) * n, lanes(k)] = back(S_, upstream, part(skips, j), masks[j], k)
        s.gathered[...] += tm(sources, s.skip[...])
        s.upstream[rows(r), 0:ci] = mm(s.skip[...], s.start_rows[0:c, :])
        excited_back(r, add, add_image, B_, s.middle, 0)

    *sums_b, dscaling_sums = over(2, 1, branch_back)
    jobs[0].settle()
    excite_backward_start(3, 0, one, dscaling_sums)
    sum_start(BACK_B, sums_b)
    s.stage[at.shortcut : at.shortcut + ci, :] = s.gathered[0:ci, :].astype(BF16)
    product_grad(lambda span: s.excited_one[:, span], c, at.output)
    jobs[0].exchange()
    gates_wait(0, 3)
    excite_backward(3, one, 0)
    s.stage[at.biases : at.biases + 16, :] = s.biases[...].astype(BF16)
    jobs[0].gather()
    jobs[1].swap()
    set_back(B_, *finish_gate(BACK_B, 0), inv_out, GROUP_G)

    def put_middle(r, j, k, dz):
        s.frame[r, j, :, lanes(k)] = dz

    gate_back(B_, 0, 3, s.middle, put_middle)
    corners = corner_copies(s.frame)
    for copy in corners:
        copy.start()

    def all_one(ky, kx, q):
        return jnp.concatenate(
            [s.active[2 * i + ky, 2 * j + kx, :, quarter(q)] for i in range(r_out) for j in range(r_out)], axis=0
        )

    kernel_grad(lambda q: s.frame[outer, outer, :, quarter(q)].reshape(points, LANES), all_one, at.group)
    jobs[0].hand()
    jobs[1].scatter()
    jobs[2].swap()
    for copy in corners:
        copy.wait_recv()

    @pl.when(ha == d.ha - 1)
    def _():
        s.frame[r_out] = blank

    @pl.when(wa == d.wa - 1)
    def _():
        s.frame[:, r_out] = blank

    meets = {0: ((1, 0),), 1: ((0, 1), (2, 0))}
    parities = [(ph, pw) for ph in range(2) for pw in range(2)]

    def entry_sums(i, add):
        for ph, pw in parities:
            first, last = PARITY_SPANS[ph, pw]
            sources = strided(i, ph, pw)
            for k in range(halves):
                windows = [
                    s.frame[i + dr, pl.ds(dc, r_out), :, lanes(k)].reshape(block, half)
                    for _, dr in meets[ph]
                    for _, dc in meets[pw]
                ]
                window = windows[0] if len(windows) == 1 else jnp.concatenate(windows, axis=1)
                dactive = mm(window, s.taps[k, first * half : last * half, :])
                fields = mm(sources, s.entry_rows[:, lanes(k)])
                for j in range(r_out):
                    field = part(fields, j)
                    _, slope = silu_and_slope(field * keep(A_, 2, k))
                    mask = mask_at(row0 + 2 * i + ph, col0 + 2 * j + pw, half, 0.5)
                    upstream = part(dactive, j) * mask * slope
                    s.active[2 * i + ph + 1, 2 * j + pw + 1, :, lanes(k)] = upstream.astype(BF16)
                    add(0, k, upstream)
                    add(1, k, upstream * field)

    sums_e = over_rows(2, entry_sums)
    jobs[1].settle()
    sum_start(BACK_A, sums_e)
    jobs[1].exchange()
    jobs[2].scatter()
    s.gathered[...] = jnp.zeros((ca, c), F32)

    def meet(h):
        upstream = s.active[h + 1, pl.ds(1, h_in)].reshape(h_in * n, c)
        s.gathered[...] += tm(s.x[h].reshape(h_in * n, ca), upstream)

    each_row(meet, h_in)
    set_back(A_, *sum_finish(BACK_A), inv_in, ENTRY_G, raised)

    kernel_rows = s.entry_kernel[...].astype(F32)
    folded = jnp.concatenate([kernel_rows * keep(A_, 6), below([keep(A_, 7)])], axis=0)
    s.stage[at.entry : at.entry + ci, :] = (
        s.gathered[0:ci, :] * keep(A_, 5) + exact(mm, s.gram[0:ci, :], folded)
    ).astype(BF16)
    jobs[3].scatter()
    s.start_rows[0:c, :] = (kernel_rows * keep(A_, 5)).T.astype(BF16)
    high, low = in_parts(fine(mt, folded, s.entry_kernel[...]), 2)
    s.start_rows[c : c + ca, :] = high
    s.start_rows[c + ca : c + 2 * ca, :] = low
    jobs[1].gather()
    jobs[2].exchange()

    def store_row(h):
        return pltpu.make_async_copy(s.raw.at[h % depth], s.images_grad.at[h], s.load_sems.at[h % depth])

    def start_back(i):
        for ph in range(2):
            h = 2 * i + ph

            @pl.when(h >= depth)
            def _(h=h):
                store_row(h - depth).wait()

            for q in range(2):
                span = pl.ds(r_out * q, r_out)
                upstream = s.active[h + 1, pl.ds(1 + r_out * q, r_out)].reshape(block, c)
                x = s.x[h, span].reshape(block, ca)
                dstart = mm(jnp.concatenate([upstream, x, x], axis=1), s.start_rows[...])
                for j in range(r_out):
                    w = r_out * q + j
                    value = part(dstart, j)
                    if ph == 0 and w % 2 == 0:
                        value = value + s.upstream[spot(i, w // 2), 0:ci]
                    s.raw[h % depth, w] = value.astype(BF16)
            store_row(h).start()

    each_row(start_back, 2)
    jobs[3].exchange()
    jobs[1].hand()
    jobs[2].gather()
    each_row(start_back, r_out, 2)
    jobs[3].gather()
    jobs[2].hand()
    jobs[3].hand()


    for copy in rims + ring + ring_back + corners:
        copy.wait_send()
    for k in range(len(VECTORS)):
        sum_wait(k, 0)
        sum_wait_across(k, 2)
    for j in range(4):
        tiles_wait(j, 0)
    for which in range(2):
        gates_wait(which, 2)
        img_wait(which, 0)
    for h in range(h_in - depth, h_in):
        store_row(h).wait()
    for job in jobs:
        job.finish()


def run(d, operands):
    n, c, ci, r = d.images, d.channels, d.inputs, d.rows
    points, h_in, group = r * r * n, 2 * r, n // d.ha
    plane = d.ha * d.wa
    half = min(256, c)
    vm = functools.partial(pl.BlockSpec, memory_space=pltpu.VMEM)
    anywhere = functools.partial(pl.BlockSpec, memory_space=pl.ANY)
    smem = functools.partial(pl.BlockSpec, memory_space=pltpu.SMEM)
    inputs = dict(
        images=anywhere(), cotangent=anywhere(), classes=vm(), image_counts=smem(),
        **{name: anywhere() for name, _ in d.vectors},
        entry_kernel=vm(), group_kernel=vm(), squeeze=vm(), excite=vm(), output_kernel=vm(), shortcut_kernel=vm(),
        second_kernel=vm(), spatial_kernel=vm(), reduce=vm(), expand=vm(), final_kernel=vm(),
    )
    outputs = dict(
        activations=(jax.ShapeDtypeStruct((r, r, n, c), BF16), anywhere()),
        images_grad=(jax.ShapeDtypeStruct((h_in, h_in, n, ci), BF16), anywhere()),
        stage=(jax.ShapeDtypeStruct((d.grad_lines, c), BF16), vm()),
        vectors=(jax.ShapeDtypeStruct((16, c), F32), vm()),
    )
    dma = pltpu.SemaphoreType.DMA
    narrow = -(-2 * (c // LANES) // 8) * 8
    last = d.jobs[3][1] // d.ha
    sums, lines = len(VECTORS), d.grad_lines // (2 * d.ha) + last // 2
    scratch = dict(
        x=pltpu.VMEM((h_in, h_in, n, d.augmented), BF16),
        raw=pltpu.VMEM((2, h_in, n, ci), BF16),
        rim=pltpu.VMEM((2, h_in, n, ci), BF16),
        rim_corner=pltpu.VMEM((1, n, ci), BF16),
        rim_rows=pltpu.VMEM((r, n, d.augmented), BF16),
        active=pltpu.VMEM((h_in + 1, h_in + 1, n, c), BF16),
        cot=pltpu.VMEM((r, r, n, c), BF16),
        middle=pltpu.VMEM((points, c), BF16),
        branch=pltpu.VMEM((points, c), BF16),
        second=pltpu.VMEM((points, c), BF16),
        excited_one=pltpu.VMEM((points, c), BF16),
        residual=pltpu.VMEM((r + 2, r + 2, n, c), BF16),
        frame=pltpu.VMEM((r + 2, r + 2, n, c), BF16),
        spatial=pltpu.VMEM((points, c), BF16),
        excited_two=pltpu.VMEM((max(points, d.grad_lines - d.jobs[2][0]), c), BF16),
        field=pltpu.VMEM((points, c), F32),
        upstream=pltpu.VMEM((points, c), F32),
        dframe=pltpu.VMEM((r + 2, r + 2, n, c), BF16),
        skip=pltpu.VMEM((r * n, c), BF16),
        turned=pltpu.VMEM((c // LANES, LANES, points), BF16),
        taps=pltpu.VMEM((c // half, 9 * half, half), BF16),
        entry_rows=pltpu.VMEM((d.augmented, c), BF16),
        short_rows=pltpu.VMEM((d.augmented, c), BF16),
        start_rows=pltpu.VMEM((c + 2 * d.augmented, ci), BF16),
        gram=pltpu.VMEM((d.augmented, d.augmented), F32),
        square_t=pltpu.VMEM((c, c), BF16),
        gathered=pltpu.VMEM((d.augmented, c), F32),
        biases=pltpu.VMEM((16, c), F32),
        vec=pltpu.VMEM((24, c), F32),
        lim=pltpu.VMEM((n, LANES), jnp.int32),
        invpix=pltpu.VMEM((d.ha, group, LANES), F32),
        keep=pltpu.VMEM((56, c), F32),
        slots=pltpu.VMEM((sums, plane, narrow, LANES), F32),
        across=pltpu.VMEM((sums, d.img, narrow, LANES), F32),
        slots_wide=pltpu.VMEM((2, plane, 2 * narrow, LANES), F32),
        across_wide=pltpu.VMEM((2, d.img, 2 * narrow, LANES), F32),
        reduced=pltpu.VMEM((16, LANES), F32),
        tile_slots=pltpu.VMEM((4, plane, n, LANES), BF16),
        dlogit=pltpu.VMEM((n, c), F32),
        gate_src=pltpu.VMEM((d.ha, 2, group, c), BF16),
        gate_slots=pltpu.VMEM((plane, 2, group, c), BF16),
        shared=pltpu.VMEM((4, d.ha, group, c), F32),
        gates=pltpu.VMEM((2, d.ha, 2, group, c), F32),
        group_x=pltpu.VMEM((2, d.img, narrow, LANES), F32),
        pooled_one=pltpu.VMEM((n, c), F32),
        before_one=pltpu.VMEM((n, d.hidden_one), F32),
        pooled_two=pltpu.VMEM((n, c), F32),
        before_two=pltpu.VMEM((n, d.hidden_two), F32),
        swaps=pltpu.VMEM((d.grad_lines // 2, c), BF16),
        scattered=pltpu.VMEM((plane, lines, LANES), BF16),
        crossed=pltpu.VMEM((d.img // 2, lines, LANES), BF16),
        crossed_all=pltpu.VMEM((d.img, last, LANES), BF16),
        summed=pltpu.VMEM((lines, LANES), BF16),
        load_sems=dma((2,)),
        vec_sems=dma((len(d.vectors),)),
        cot_sem=dma((2,)),
        sum_sems=dma((sums, 4)),
        tile_sems=dma((4, 2)),
        gate_sems=dma((2, 4)),
        group_sems=dma((2, 2)),
        ring_send=dma((2, 8)),
        ring_recv=dma((2, 8)),
        rim_send=dma((3,)),
        rim_recv=dma((3,)),
        corner_send=dma((3,)),
        corner_recv=dma((3,)),
        grad_sems=dma((len(d.jobs), 10)),
    )
    d.names = [*inputs, *outputs, *scratch]
    return pl.pallas_call(
        functools.partial(kernel, d),
        out_shape=[shape for shape, _ in outputs.values()],
        in_specs=list(inputs.values()),
        out_specs=[spec for _, spec in outputs.values()],
        scratch_shapes=list(scratch.values()),
        compiler_params=pltpu.CompilerParams(
            collective_id=0, has_side_effects=True, vmem_limit_bytes=d.vmem, fuse_transposed_lhs_in_matmul=True
        ),
        name="blocks",
    )(*[operands[name] for name in inputs])


def widen(d, activations, images_grad, total, sums):
    names = [name for name, (_, size) in d.grad_rows.items() if size != 16]
    first_bias = [first for first, size in d.grad_rows.values() if size == 16][0]
    c, nch = d.channels, d.channels // LANES
    vectors = sums.shape[0]
    bias_sizes = (c, LANES, c, LANES)

    def shape_of(name):
        return (c, d.hidden_two) if name == d.chunked else (d.grad_rows[name][1], c)

    def widen_kernel(activations_in, images_in, total_in, sums_in, *refs):
        outs, (large_a, large_b, biases, sems, vec_sems) = refs[:-5], refs[-5:]
        activations_out, images_out, *rest = outs
        grads, lines = rest[: len(names)], rest[len(names) :]
        arriving = [
            pltpu.make_async_copy(images_in, large_a, sems.at[0]),
            pltpu.make_async_copy(activations_in, large_b, sems.at[1]),
        ]
        leaving = [
            pltpu.make_async_copy(large_a, images_out, sems.at[2]),
            pltpu.make_async_copy(large_b, activations_out, sems.at[3]),
        ]
        for copy in arriving:
            copy.start()
        biases[...] = total_in[first_bias : first_bias + 16, :].astype(F32)
        sources = [sums_in.at[i] for i in range(vectors)]
        sources += [biases.at[i, pl.ds(0, size)] for i, size in enumerate(bias_sizes)]
        small = [
            pltpu.make_async_copy(source, line, vec_sems.at[i])
            for i, (source, line) in enumerate(zip(sources, lines, strict=True))
        ]
        for copy in small:
            copy.start()
        for into, out in zip(arriving, leaving, strict=True):
            into.wait()
            out.start()
        for name, out in zip(names, grads, strict=True):
            first, size = d.grad_rows[name]
            if name == d.chunked:
                for i in range(nch):
                    chunk = total_in[first : first + size, i * LANES : (i + 1) * LANES]
                    out[i * LANES : (i + 1) * LANES, :] = chunk.astype(F32)
            else:
                out[...] = total_in[first : first + size, :].astype(F32)
        for copy in small + leaving:
            copy.wait()

    anywhere = pl.BlockSpec(memory_space=pl.ANY)
    inside = pl.BlockSpec(memory_space=pltpu.VMEM)
    line_sizes = (c,) * vectors + bias_sizes
    out = pl.pallas_call(
        widen_kernel,
        out_shape=[
            jax.ShapeDtypeStruct(activations.shape, BF16), jax.ShapeDtypeStruct(images_grad.shape, BF16),
            *[jax.ShapeDtypeStruct(shape_of(name), F32) for name in names],
            *[jax.ShapeDtypeStruct((size,), F32) for size in line_sizes],
        ],
        in_specs=[anywhere, anywhere, inside, inside],
        out_specs=[anywhere, anywhere, *[inside] * len(names), *[anywhere] * len(line_sizes)],
        scratch_shapes=[
            pltpu.VMEM(images_grad.shape, BF16), pltpu.VMEM(activations.shape, BF16), pltpu.VMEM((16, c), F32),
            pltpu.SemaphoreType.DMA((4,)), pltpu.SemaphoreType.DMA((len(line_sizes),)),
        ],
        compiler_params=pltpu.CompilerParams(vmem_limit_bytes=d.vmem),
        name="widen",
    )(activations, images_grad, total, sums)
    grads, lines = out[2 : 2 + len(names)], out[2 + len(names) :]
    return out[0], out[1], types.SimpleNamespace(**dict(zip(names, grads, strict=True))), lines


def body(
    images, classes, image_counts, entry_kernel, entry_gain, entry_shift, group_kernel, group_gain, group_shift,
    squeeze_weight, squeeze_bias, excite_weight, excite_bias, output_kernel, output_gain, output_shift,
    shortcut_kernel, shortcut_gain, shortcut_shift, second_kernel, second_gain, second_shift, spatial_kernel,
    spatial_gain, spatial_shift, reduce_weight, reduce_bias, expand_weight, expand_bias, final_kernel, final_gain,
    final_shift, cotangent,
):
    vectors = dict(
        entry_gain=entry_gain, entry_shift=entry_shift, group_gain=group_gain, group_shift=group_shift,
        output_gain=output_gain, output_shift=output_shift, shortcut_gain=shortcut_gain,
        shortcut_shift=shortcut_shift, second_gain=second_gain, second_shift=second_shift,
        spatial_gain=spatial_gain, spatial_shift=spatial_shift, final_gain=final_gain, final_shift=final_shift,
        excite_bias=excite_bias, expand_bias=expand_bias,
        squeeze_bias=jnp.pad(squeeze_bias, (0, -squeeze_bias.shape[0] % LANES)), reduce_bias=reduce_bias,
    )
    d = types.SimpleNamespace(
        ha=lax.axis_size("ha"), wa=lax.axis_size("wa"), img=lax.axis_size("img"),
        images=images.shape[0], rows=images.shape[1] // 2, inputs=images.shape[3],
        channels=entry_kernel.shape[1], width=group_kernel.shape[2],
        hidden_one=squeeze_weight.shape[1], hidden_two=reduce_weight.shape[1], vmem=64 * 1024 * 1024 - 65536,
        vectors=[(name, v.shape[0]) for name, v in vectors.items()],
    )
    n, c = d.images, d.channels
    d.grad_rows, d.jobs, d.grad_lines = grad_rows(c, d.inputs, d.hidden_one, d.hidden_two, d.width)
    d.augmented = -(-(d.inputs + 3) // LANES) * LANES
    d.chunked = list(d.grad_rows)[1]
    operands = dict(
        **vectors,
        images=images.transpose(1, 2, 0, 3),
        cotangent=cotangent.transpose(1, 2, 0, 3),
        classes=classes.reshape(d.img, n),
        image_counts=image_counts,
        entry_kernel=entry_kernel,
        group_kernel=group_kernel.reshape(9, d.width, c),
        squeeze=squeeze_weight.T,
        excite=excite_weight,
        output_kernel=output_kernel,
        shortcut_kernel=shortcut_kernel,
        second_kernel=second_kernel,
        spatial_kernel=spatial_kernel.reshape(9, d.width, c),
        reduce=reduce_weight,
        expand=expand_weight,
        final_kernel=final_kernel,
    )
    activations, images_grad, total, sums = run(d, operands)
    activations, images_grad, g, lines = widen(d, activations, images_grad, total, sums)
    biases = lines[-4:]

    def taps_of(v):
        return v.reshape(3, 3, d.width, c)

    def pair(i):
        return lines[i], lines[i + 1]

    return (
        activations.transpose(2, 0, 1, 3),
        images_grad.transpose(2, 0, 1, 3),
        g.entry, *pair(ENTRY_G),
        taps_of(g.group), *pair(GROUP_G),
        g.squeeze.T, biases[1][: d.hidden_one], g.excite, biases[0],
        g.output, *pair(OUTPUT_G),
        g.shortcut, *pair(SHORT_G),
        g.second, *pair(SECOND_G),
        taps_of(g.spatial), *pair(SPATIAL_G),
        g.reduce, biases[3][: d.hidden_two], g.expand, biases[2],
        g.final, *pair(FINAL_G),
    )


def solution(mesh):
    spread = P("img", "ha", "wa", None)
    return jax.shard_map(
        body,
        mesh=mesh,
        in_specs=(spread, *[P()] * 31, spread),
        out_specs=(spread, spread, *[P()] * 29),
        check_vma=False,
    )
```

time: 2250 us -> 289 us (0.13)
  blocking collectives: 768 us -> 0 us
  waiting for transfers between devices: 454 us -> 0 us
  local copies, waits for them, and re-layouts: 428 us -> 2.52 us
  other arithmetic: 302 us -> 0 us
  Pallas kernels: 0 us -> 286 us
  matrix products: 246 us -> 0 us
    psum x12 -> x0, blocking collectives: 768 us -> none  [the longest x6 389 us: moments(): totals, squares = lax.psum((totals, squares), ('ha', 'wa', 'img'))]
    psum x5 -> x0, waiting for transfers between devices: 401 us -> none  [the longest x4 260 us: image_sums(): lax.psum(jnp.sum(field, axis=(1, 2)).astype(jnp.bfloat16), ('ha', 'wa'))]
    pallas_call x0 -> x2, Pallas kernels: none -> 286 us  [the longest x1 276 us: run(): pl.pallas_call(functools.partial(kernel, d), out_shape=[shape for shape,...]
    dot_general x81 -> x0, matrix products: 246 us -> none  [the longest x27 117 us: taps(): jnp.einsum(formula, window, kernel[tap_row, tap_col], preferred_element_t...]
    scatter-add x12 -> x0, other arithmetic: 172 us -> none  [the longest x9 163 us: spread(): canvas = canvas.at[:, tap_row:tap_row + 2 * rows_out - 1:2, tap_col:tap_c...]
    reshape x16 -> x1, local copies, waits for them, and re-layouts: 118 us -> 1.35 us  [body(): classes.reshape(d.img, n)]
    slice x16 -> x0, local copies, waits for them, and re-layouts: 112 us -> none  [the longest x3 72.1 us: taps(): field[:, tap_row:tap_row + stride * (rows_out - 1) + 1:stride, tap_col:ta...]
    transpose x9 -> x0, local copies, waits for them, and re-layouts: 77.9 us -> none  [spread(): jnp.einsum(BACKWARD, gradient, kernel[tap_row, tap_col], preferred_elemen...]
  transfers between devices with their start and end apart: 17 -> 0, of which waited for: 16 -> 0; matrix products, arithmetic and copies ran while one was open for 6% -> 0% of each run, Pallas kernels for 0% -> 0%
where the time goes in v1:
time: 289 us
  Pallas kernels  286 us (99%)
    pallas_call x1, Pallas kernels, run(): pl.pallas_call(functools.partial(kernel, d), out_shape=[shape for shape,...  276 us
    pallas_call x1, Pallas kernels, widen(): pl.pallas_call(widen_kernel, out_shape=[jax.ShapeDtypeStruct(activations....  9.42 us

profile of v1, /device:TPU:0, one launch (start us, length us, event | category | flops | bytes accessed | tf_op | source)
XLA Modules:
  0.0 289.1 jit_solution(8790553583744379916)
XLA Ops:
  0.7 1.2 pad.4.refs_20_
  1.8 1.3 reshape.77.refs_2_
  3.2 276.3 %blocks.1 = (bf16[5,5,64,512]{3,2,1,0:T(8,128)(2,1)}, bf16[10,10,64,192]{3,2,1,0:T(8,128)(2,1)}, bf16[3712,512]{1,0:T(8,128)(2,1)}, f32[16,512]{1,0:T(8,128)}) custom-call(bf16[10,10,64,192]{3,2,1,0:T(8,128)(2,1)} %bitcast.11, bf16[5,5,64,512]{3,2,1,0:T(8,128)(2,1)} %bitcast.12, s32[8,64]{1,0:T(8,128)} %reshape.77.refs_2_, s32[8]{0:T(128)} %refs_3_.1, ...), custom_call_target="tpu_custom_call" | custom-call | tf_op jit(solution)/shard_map/blocks/pallas_call | solution.py:1374
  279.5 9.4 %widen.1 = (bf16[5,5,64,512]{3,2,1,0:T(8,128)(2,1)}, bf16[10,10,64,192]{3,2,1,0:T(8,128)(2,1)}, f32[512,512]{1,0:T(8,128)}, f32[512,128]{1,0:T(8,128)}, f32[128,...) custom-call(bf16[5,5,64,512]{3,2,1,0:T(8,128)(2,1)} %get-tuple-eleme, ...), custom_call_target="tpu_custom_call" | custom-call | tf_op jit(solution)/shard_map/widen/pallas_call | solution.py:1437

commit v2 on v1

--- a/solution.py
+++ b/solution.py
@@ -14,6 +14,7 @@
 MESH = pl.DeviceIdType.MESH
 FAR = 1 << 20
 LANES = 128
+SENT = "_sent"
 
 (
     ENTRY_G, ENTRY_S, GROUP_G, GROUP_S, OUTPUT_G, OUTPUT_S, SHORT_G, SHORT_S, SECOND_G, SECOND_S,
@@ -726,6 +727,12 @@
         load(h).start()
     cot_load = pltpu.make_async_copy(s.cotangent, s.cot, s.cot_sem.at[0])
     cot_load.start()
+    weight_loads = [
+        pltpu.make_async_copy(getattr(s, name + SENT), getattr(s, name), s.weight_sems.at[i])
+        for i, name in enumerate(d.weights)
+    ]
+    for copy in weight_loads:
+        copy.start()
     vec_loads = [
         pltpu.make_async_copy(getattr(s, name), s.vec.at[i, pl.ds(0, size)], s.vec_sems.at[i])
         for i, (name, size) in enumerate(d.vectors)
@@ -759,11 +766,6 @@
     s.invpix[...] = (1.0 / (sides * sides)).reshape(d.ha, group, LANES)
     s.biases[...] = jnp.zeros((16, c), F32)
 
-    pl.semaphore_wait(barrier, plane - 1 + d.img - 1)
-    rims = rim_copies()
-    for copy in rims:
-        copy.start()
-
     s.gram[...] = jnp.zeros((ca, ca), F32)
     s.gathered[:, 0:ca] = jnp.zeros((ca, ca), F32)
 
@@ -782,9 +784,16 @@
         x = strided(i, 0, 0)
         s.gathered[:, 0:ca] += tm(x, x)
 
-    each_row(load_rows)
+    each_row(load_rows, 2)
+    pl.semaphore_wait(barrier, plane - 1 + d.img - 1)
+    rims = rim_copies()
+    for copy in rims:
+        copy.start()
+    each_row(load_rows, r_out, 2)
     sums_a = gram_moments(s.gram, s.entry_kernel)
     sum_start(SUM_A, sums_a + gram_moments(s.gathered, s.shortcut_kernel))
+    for copy in weight_loads:
+        copy.wait()
     build_kernel(s.group_kernel)
     s.entry_rows[0:ci, :] = s.entry_kernel[...]
     s.short_rows[0:ci, :] = s.shortcut_kernel[...]
@@ -860,16 +869,23 @@
 
     def gated_sums(m, store):
         def row(r, add, add_image):
-            masks, masks_half = masks_out(r), masks_out(r, 0.5)
+            masks = masks_out(r)
+            for j, k in pieces:
+                add_image(0, k, gated(m, store, r, j, k, masks[j]))
+
+        return over(0, 1, row)[0]
+
+    def slope_sums(m, store):
+        def row(r, add, add_image):
+            masks_half = masks_out(r, 0.5)
             for j, k in pieces:
                 field = store[spot(r, j), lanes(k)].astype(F32)
-                value, slope = silu_and_slope(field * keep(m, 2, k) + keep(m, 3, k))
+                _, slope = silu_and_slope(field * keep(m, 2, k) + keep(m, 3, k))
                 slope = slope * masks_half[j]
-                add_image(0, k, value * masks[j])
-                add_image(1, k, slope)
-                add_image(2, k, slope * field)
-
-        return over(0, 3, row)
+                add_image(0, k, slope)
+                add_image(1, k, slope * field)
+
+        return over(0, 2, row)
 
     def excite_row(r, m, store, forward, excited):
         masks = masks_out(r)
@@ -877,9 +893,7 @@
             value = gated(m, store, r, j, k, masks[j]) * every(forward, k)
             excited[spot(r, j), lanes(k)] = value.astype(BF16)
 
-    pooled_sums, *gate_sums = gated_sums(B_, s.middle)
-    excite_forward(0, one, pooled_sums)
-    gates_load(gate_sums)
+    excite_forward(0, one, gated_sums(B_, s.middle))
 
     def branch_row(r, add):
         excite_row(r, B_, s.middle, 0, s.excited_one)
@@ -890,6 +904,7 @@
             add(1, k, field * field)
 
     sum_start(SUM_C, over_rows(2, branch_row))
+    gates_load(slope_sums(B_, s.middle))
     set_norm(C_, *sum_finish(SUM_C), inv_out, OUTPUT_G, OUTPUT_S)
 
 
@@ -952,9 +967,7 @@
     gates_finish(0)
     set_norm(E_, *sum_finish(SUM_E), inv_out, SPATIAL_G, SPATIAL_S)
 
-    pooled_sums, *gate_sums = gated_sums(E_, s.spatial)
-    excite_forward(1, two, pooled_sums)
-    gates_load(gate_sums)
+    excite_forward(1, two, gated_sums(E_, s.spatial))
 
     def final_row(r, add):
         excite_row(r, E_, s.spatial, 1, s.excited_two)
@@ -967,6 +980,7 @@
     sum_start(SUM_F, over_rows(2, final_row))
     cot_load.wait()
     build_turned(s.spatial_kernel, range(9))
+    gates_load(slope_sums(E_, s.spatial))
     set_norm(F_, *sum_finish(SUM_F), inv_out, FINAL_G, FINAL_S)
     gates_start(1)
 
@@ -1288,8 +1302,7 @@
     inputs = dict(
         images=anywhere(), cotangent=anywhere(), classes=vm(), image_counts=smem(),
         **{name: anywhere() for name, _ in d.vectors},
-        entry_kernel=vm(), group_kernel=vm(), squeeze=vm(), excite=vm(), output_kernel=vm(), shortcut_kernel=vm(),
-        second_kernel=vm(), spatial_kernel=vm(), reduce=vm(), expand=vm(), final_kernel=vm(),
+        entry_kernel=vm(), shortcut_kernel=vm(), **{name + SENT: anywhere() for name in d.weights},
     )
     outputs = dict(
         activations=(jax.ShapeDtypeStruct((r, r, n, c), BF16), anywhere()),
@@ -1355,6 +1368,8 @@
         crossed=pltpu.VMEM((d.img // 2, lines, LANES), BF16),
         crossed_all=pltpu.VMEM((d.img, last, LANES), BF16),
         summed=pltpu.VMEM((lines, LANES), BF16),
+        **{name: pltpu.VMEM(value.shape, BF16) for name, value in d.weights.items()},
+        weight_sems=dma((len(d.weights),)),
         load_sems=dma((2,)),
         vec_sems=dma((len(d.vectors),)),
         cot_sem=dma((2,)),
@@ -1394,8 +1409,10 @@
     def shape_of(name):
         return (c, d.hidden_two) if name == d.chunked else (d.grad_rows[name][1], c)
 
-    def widen_kernel(activations_in, images_in, total_in, sums_in, *refs):
-        outs, (large_a, large_b, biases, sems, vec_sems) = refs[:-5], refs[-5:]
+    def widen_kernel(activations_in, images_in, total_sent, sums_in, *refs):
+        outs, (total, *wide), (large_a, large_b, biases, sems, vec_sems, grad_sems) = (
+            refs[: -len(names) - 7], refs[-len(names) - 7 : -6], refs[-6:]
+        )
         activations_out, images_out, *rest = outs
         grads, lines = rest[: len(names)], rest[len(names) :]
         arriving = [
@@ -1406,9 +1423,12 @@
             pltpu.make_async_copy(large_a, images_out, sems.at[2]),
             pltpu.make_async_copy(large_b, activations_out, sems.at[3]),
         ]
+        total_copy = pltpu.make_async_copy(total_sent, total, sems.at[4])
+        total_copy.start()
         for copy in arriving:
             copy.start()
-        biases[...] = total_in[first_bias : first_bias + 16, :].astype(F32)
+        total_copy.wait()
+        biases[...] = total[first_bias : first_bias + 16, :].astype(F32)
         sources = [sums_in.at[i] for i in range(vectors)]
         sources += [biases.at[i, pl.ds(0, size)] for i, size in enumerate(bias_sizes)]
         small = [
@@ -1417,18 +1437,22 @@
         ]
         for copy in small:
             copy.start()
-        for into, out in zip(arriving, leaving, strict=True):
-            into.wait()
-            out.start()
-        for name, out in zip(names, grads, strict=True):
+        grad_copies = []
+        for i, (name, held, out) in enumerate(zip(names, wide, grads, strict=True)):
             first, size = d.grad_rows[name]
             if name == d.chunked:
-                for i in range(nch):
-                    chunk = total_in[first : first + size, i * LANES : (i + 1) * LANES]
-                    out[i * LANES : (i + 1) * LANES, :] = chunk.astype(F32)
+                for q in range(nch):
+                    chunk = total[first : first + size, q * LANES : (q + 1) * LANES]
+                    held[q * LANES : (q + 1) * LANES, :] = chunk.astype(F32)
             else:
-                out[...] = total_in[first : first + size, :].astype(F32)
-        for copy in small + leaving:
+                held[...] = total[first : first + size, :].astype(F32)
+            grad_copies.append(pltpu.make_async_copy(held, out, grad_sems.at[i]))
+            grad_copies[-1].start()
+            if i == 1:
+                for into, onward in zip(arriving, leaving, strict=True):
+                    into.wait()
+                    onward.start()
+        for copy in small + leaving + grad_copies:
             copy.wait()
 
     anywhere = pl.BlockSpec(memory_space=pl.ANY)
@@ -1441,11 +1465,13 @@
             *[jax.ShapeDtypeStruct(shape_of(name), F32) for name in names],
             *[jax.ShapeDtypeStruct((size,), F32) for size in line_sizes],
         ],
-        in_specs=[anywhere, anywhere, inside, inside],
-        out_specs=[anywhere, anywhere, *[inside] * len(names), *[anywhere] * len(line_sizes)],
+        in_specs=[anywhere, anywhere, anywhere, inside],
+        out_specs=[anywhere] * (2 + len(names) + len(line_sizes)),
         scratch_shapes=[
+            pltpu.VMEM(total.shape, BF16), *[pltpu.VMEM(shape_of(name), F32) for name in names],
             pltpu.VMEM(images_grad.shape, BF16), pltpu.VMEM(activations.shape, BF16), pltpu.VMEM((16, c), F32),
-            pltpu.SemaphoreType.DMA((4,)), pltpu.SemaphoreType.DMA((len(line_sizes),)),
+            pltpu.SemaphoreType.DMA((5,)), pltpu.SemaphoreType.DMA((len(line_sizes),)),
+            pltpu.SemaphoreType.DMA((len(names),)),
         ],
         compiler_params=pltpu.CompilerParams(vmem_limit_bytes=d.vmem),
         name="widen",
@@ -1480,23 +1506,21 @@
     d.grad_rows, d.jobs, d.grad_lines = grad_rows(c, d.inputs, d.hidden_one, d.hidden_two, d.width)
     d.augmented = -(-(d.inputs + 3) // LANES) * LANES
     d.chunked = list(d.grad_rows)[1]
+    d.weights = dict(
+        group_kernel=group_kernel.reshape(9, d.width, c), squeeze=squeeze_weight.T, excite=excite_weight,
+        output_kernel=output_kernel, second_kernel=second_kernel,
+        spatial_kernel=spatial_kernel.reshape(9, d.width, c), reduce=reduce_weight, expand=expand_weight,
+        final_kernel=final_kernel,
+    )
     operands = dict(
         **vectors,
+        **{name + SENT: value for name, value in d.weights.items()},
         images=images.transpose(1, 2, 0, 3),
         cotangent=cotangent.transpose(1, 2, 0, 3),
         classes=classes.reshape(d.img, n),
         image_counts=image_counts,
         entry_kernel=entry_kernel,
-        group_kernel=group_kernel.reshape(9, d.width, c),
-        squeeze=squeeze_weight.T,
-        excite=excite_weight,
-        output_kernel=output_kernel,
         shortcut_kernel=shortcut_kernel,
-        second_kernel=second_kernel,
-        spatial_kernel=spatial_kernel.reshape(9, d.width, c),
-        reduce=reduce_weight,
-        expand=expand_weight,
-        final_kernel=final_kernel,
     )
     activations, images_grad, total, sums = run(d, operands)
     activations, images_grad, g, lines = widen(d, activations, images_grad, total, sums)

time: 289 us -> 286 us (0.990)
  Pallas kernels: 286 us -> 282 us
where the time goes in v2:
time: 286 us; the launch traced here: 285 us
  Pallas kernels  282 us (99%)
    pallas_call x1, Pallas kernels, run(): pl.pallas_call(functools.partial(kernel, d), out_shape=[shape for shape,...  274 us
    pallas_call x1, Pallas kernels, widen(): pl.pallas_call(widen_kernel, out_shape=[jax.ShapeDtypeStruct(activations....  8.13 us

profile of v2, /device:TPU:0, one launch (start us, length us, event | category | flops | bytes accessed | tf_op | source)
XLA Modules:
  0.0 285.5 jit_solution(1104123334631322072)
XLA Ops:
  0.7 1.2 pad.4.refs_20_
  1.8 1.3 reshape.77.refs_2_
  3.2 274.0 %blocks.1 = (bf16[5,5,64,512]{3,2,1,0:T(8,128)(2,1)}, bf16[10,10,64,192]{3,2,1,0:T(8,128)(2,1)}, bf16[3712,512]{1,0:T(8,128)(2,1)}, f32[16,512]{1,0:T(8,128)}) custom-call(bf16[10,10,64,192]{3,2,1,0:T(8,128)(2,1)} %bitcast.11, bf16[5,5,64,512]{3,2,1,0:T(8,128)(2,1)} %bitcast.12, s32[8,64]{1,0:T(8,128)} %reshape.77.refs_2_, s32[8]{0:T(128)} %refs_3_.1, ...), custom_call_target="tpu_custom_call" | custom-call | tf_op jit(solution)/shard_map/blocks/pallas_call | solution.py:1389
  277.1 8.1 %widen.1 = (bf16[5,5,64,512]{3,2,1,0:T(8,128)(2,1)}, bf16[10,10,64,192]{3,2,1,0:T(8,128)(2,1)}, f32[512,512]{1,0:T(8,128)}, f32[512,128]{1,0:T(8,128)}, f32[128,...) custom-call(bf16[5,5,64,512]{3,2,1,0:T(8,128)(2,1)} %get-tuple-eleme, ...), custom_call_target="tpu_custom_call" | custom-call | tf_op jit(solution)/shard_map/widen/pallas_call | solution.py:1461
